TPU v7x, 512 devices: a whole 4x4x16 slice. The times are simulated.
512 devices in a mesh: section: 4 (over y_lo, core), ctx: 16 (over z), head: 8 (over x, y_hi).
Axes of the slice: x: 4, y: 4 (y_hi: 2, y_lo: 2; y = y_hi * 2 + y_lo), z: 16, core: 2. Of those that a mesh axis runs over, the one named last changes fastest.
Arguments:
- self_hidden: bfloat16 [8192, 4096], P(('section', 'ctx')), may hold values from -6 to 6
- kv_weight: bfloat16 [4096, 2048], P('section', 'head'), may hold values from -0.09375 to 0.09375
- signs: int32 [8, 128], P('head'), may hold values from -1 to 1, as said below
- positions: int32 [8192], replicated, may hold values from 0 to 8191, as said below
- queries: bfloat16 [8192, 4096], P(('section', 'ctx'), 'head'), may hold values from -112 to 112
- out_weight: bfloat16 [4096, 4096], P('head', 'section'), may hold values from -0.375 to 0.375
- query_weight: bfloat16 [4096, 4096], P('section', 'head'), may hold values from -0.09375 to 0.09375
- norm_gain: bfloat16 [4096], replicated, may hold values from 0.099609375 to 1.8984375
Outputs:
- stream: bfloat16 [8192, 4096], P(('section', 'ctx'), 'head')
- second: bfloat16 [8192, 4096], P(('section', 'ctx'), 'head')
Inputs may be any that keep to these rules, and one draw needn't show every extreme that they name: `signs`: every entry is -1 or +1. Within each aligned block of 128 tokens the positions rise by one; every position from 0 to 8191 appears exactly once.
All inputs are finite; a program needn't handle non-finite values.
Results may differ from a plain program's by a relative error of at most 0.035.
Values may be sent and summed in bfloat16 or wider, within the bound.
No kernel may reach another device: no remote copies, remote signals or barrier semaphores. Data moves between devices by JAX's collectives and lax.ppermute only.
A program may use at most 64 MiB of HBM per device.

v0:
```python
import math

import jax
import jax.numpy as jnp
from jax import lax
from jax.sharding import PartitionSpec as P

HEADS = 32
KVH = 8
HD = 128


def hadamard_table():
    indices = jnp.arange(HD, dtype=jnp.int32)
    intersection = jnp.bitwise_and(indices[:, None], indices[None, :])
    parity = jnp.zeros((HD, HD), jnp.int32)
    for bit_index in range(HD.bit_length() - 1):
        parity = parity + jnp.bitwise_and(jnp.right_shift(intersection, bit_index), 1)
    parity = jnp.bitwise_and(parity, 1)
    return (1.0 - 2.0 * parity.astype(jnp.float32)) * jnp.float32(1.0 / math.sqrt(HD))


def fold_rows(source, weight_rows):
    return jnp.dot(source, weight_rows, preferred_element_type=jnp.float32)


def attend(query_rows, cache_all, positions, query_pos):
    tok_count = query_rows.shape[0]
    kv_heads = cache_all.shape[1] // (2 * HD)
    group_size = HEADS // KVH
    key_block = 4 * tok_count
    block_count = cache_all.shape[0] // key_block
    query_heads = query_rows.reshape(tok_count, kv_heads, group_size, HD)
    cache_blocks = cache_all.reshape(block_count, key_block, kv_heads, 2, HD)
    pos_blocks = positions.reshape(block_count, key_block)
    inv_root = jnp.float32(1.0 / math.sqrt(HD))

    def absorb(running, inputs):
        highest, denominator, accumulated = running
        cache_block, pos_block = inputs
        scores = (
            jnp.einsum(
                "tkgd,skd->kgts",
                query_heads,
                cache_block[:, :, 0, :],
                preferred_element_type=jnp.float32,
            )
            * inv_root
        )
        allowed = pos_block[None, :] <= query_pos[:, None]
        scores = jnp.where(allowed[None, None], scores, -jnp.inf)
        new_high = jnp.maximum(highest, jnp.max(scores, axis=-1))
        shrink = jnp.exp(highest - new_high)
        weights = jnp.exp(scores - new_high[..., None])
        denominator = denominator * shrink + jnp.sum(weights, axis=-1)
        accumulated = accumulated * shrink[..., None] + jnp.einsum(
            "kgts,skd->kgtd",
            weights.astype(jnp.bfloat16),
            cache_block[:, :, 1, :],
            preferred_element_type=jnp.float32,
        )
        return ((new_high, denominator, accumulated), None)

    start_high = jnp.full((kv_heads, group_size, tok_count), -1e30, jnp.float32)
    start_denominator = jnp.zeros((kv_heads, group_size, tok_count), jnp.float32)
    start_accumulated = jnp.zeros((kv_heads, group_size, tok_count, HD), jnp.float32)
    (highest, denominator, accumulated), _ = lax.scan(
        absorb, (start_high, start_denominator, start_accumulated), (cache_blocks, pos_blocks)
    )
    attended = accumulated / denominator[..., None]
    return (
        jnp.transpose(attended, (2, 0, 1, 3))
        .reshape(tok_count, kv_heads * group_size * HD)
        .astype(jnp.bfloat16)
    )


def per_device(
    self_hidden, kv_weight, signs, positions, queries, out_weight, query_weight, norm_gain
):
    tok_count = self_hidden.shape[0]
    kv_heads = signs.shape[0]
    projected = fold_rows(self_hidden, lax.all_gather(kv_weight, "section", axis=0, tiled=True))
    projected = (
        projected.reshape(tok_count, kv_heads, 2, HD) * signs.astype(jnp.float32)[None, :, None, :]
    )
    rotated = jnp.einsum(
        "tkcd,de->tkce", projected, hadamard_table(), precision=lax.Precision.HIGHEST
    )
    cache_local = rotated.astype(jnp.bfloat16).reshape(tok_count, kv_heads * 2 * HD)
    cache_all = lax.all_gather(cache_local, ("section", "ctx"), axis=0, tiled=True)
    block_index = lax.axis_index("section") * lax.axis_size("ctx") + lax.axis_index("ctx")
    query_pos = lax.dynamic_slice_in_dim(positions, block_index * tok_count, tok_count, 0)
    first_layer = attend(queries, cache_all, positions, query_pos)
    partial_value = jnp.dot(
        first_layer,
        lax.all_gather(out_weight, "section", axis=1, tiled=True),
        preferred_element_type=jnp.float32,
    )
    share_width = self_hidden.shape[1] // lax.axis_size("head")
    offset = lax.axis_index("head") * share_width
    summed = lax.psum(partial_value.astype(jnp.bfloat16), "head").astype(jnp.float32)
    residual_sum = self_hidden.astype(jnp.float32) + summed
    mean_square = jnp.mean(residual_sum * residual_sum, axis=-1, keepdims=True)
    normed = (residual_sum * lax.rsqrt(mean_square + 1e-06) * norm_gain.astype(jnp.float32)).astype(
        jnp.bfloat16
    )
    own_stream = lax.dynamic_slice_in_dim(residual_sum, offset, share_width, 1)
    second_queries = fold_rows(
        normed, lax.all_gather(query_weight, "section", axis=0, tiled=True)
    ).astype(jnp.bfloat16)
    second = attend(second_queries, cache_all, positions, query_pos)
    return (own_stream.astype(jnp.bfloat16), second)


def solution(mesh):
    return jax.shard_map(
        per_device,
        mesh=mesh,
        in_specs=(
            P(("section", "ctx"), None),
            P("section", "head"),
            P("head", None),
            P(),
            P(("section", "ctx"), "head"),
            P("head", "section"),
            P("section", "head"),
            P(),
        ),
        out_specs=(P(("section", "ctx"), "head"), P(("section", "ctx"), "head")),
        check_vma=False,
    )
```

profile of v0, /device:TPU:1, one launch (start us, length us, event | category | flops | bytes accessed | tf_op | source)
XLA Modules:
  0.0 485.1 jit_solution(8114737692995512615)
XLA Ops:
  8.6 44.0 %all-gather.5.cloned.1.call-done = bf16[4096,256]{1,0:T(8,128)(2,1)} async-done(((bf16[1024,256]{1,0:T(8,128)(2,1)}), bf16[4096,256]{1,0:T(8,128)(2,1)}) %all-gather.5.cloned.1.call-update) | async-done | bytes 2097168 | tf_op jit(solution)/shard_map/all_gather | solution.py:83
  52.6 2.4 convolution_bitcast_fusion.2
  57.2 164.3 %all-gather.7.cloned.1.call-done = bf16[8192,256]{0,1:T(8,128)(2,1)} async-done(((bf16[128,256]{0,1:T(8,128)(2,1)}), bf16[8192,256]{0,1:T(8,128)(2,1)}) %all-gather.7.cloned.1.call-update) | async-done | bytes 4194320 | tf_op jit(solution)/shard_map/all_gather | solution.py:91
  221.4 6.0 %copy.28 = bf16[32,8,16,512]{3,2,1,0:T(8,128)(2,1)} copy(bf16[32,8,16,512]{3,1,2,0:T(8,128)(2,1)} %bitcast.158) | data formatting | bytes 8388608
  227.4 7.9 %copy.19 = bf16[16,512,1,2,128]{4,1,3,2,0:T(8,128)(2,1)} copy(bf16[16,512,1,2,128]{1,0,4,3,2:T(8,128)(2,1)} %bitcast.157) | data formatting | bytes 8388608
  235.3 32.7 %while.30 = (s32[]{:T(128)}, f32[1,4,128]{2,1,0:T(4,128)S(1)}, f32[1,4,128]{2,1,0:T(4,128)S(1)}, f32[1,4,128,128]{3,2,1,0:T(8,128)S(1)}, s32[16,512]{1,0:T(8,128...) while((s32[]{:T(128)}, f32[1,4,128]{2,1,0:T(4,128)S(1)}, ...), condition=%wide.region_3.4_spmd.clone, body=%wide.region_0.3_spmd.clone.sunk | while | flops 136317952 | bytes 4758137 | solution.py:67
  237.4 1.0 dynamic-slice_bitcast_fusion.4
  239.4 1.0 dynamic-slice_bitcast_fusion.4
  241.5 1.0 dynamic-slice_bitcast_fusion.4
  243.5 1.0 dynamic-slice_bitcast_fusion.4
  245.6 1.0 dynamic-slice_bitcast_fusion.4
  247.6 1.0 dynamic-slice_bitcast_fusion.4
  249.7 1.0 dynamic-slice_bitcast_fusion.4
  251.7 1.0 dynamic-slice_bitcast_fusion.4
  253.8 1.0 dynamic-slice_bitcast_fusion.4
  255.8 1.0 dynamic-slice_bitcast_fusion.4
  259.9 1.0 dynamic-slice_bitcast_fusion.4
  261.9 1.0 dynamic-slice_bitcast_fusion.4
  264.0 1.0 dynamic-slice_bitcast_fusion.4
  268.2 8.3 %all-gather.9.cloned.1.call-done = bf16[512,4096]{1,0:T(8,128)(2,1)} async-done(((bf16[512,1024]{1,0:T(8,128)(2,1)}), bf16[512,4096]{1,0:T(8,128)(2,1)}) %all-gather.9.cloned.1.call-update) | async-done | bytes 4194320 | tf_op jit(solution)/shard_map/all_gather | solution.py:97
  276.5 3.9 convolution_convert_fusion
  281.1 99.3 %all-reduce.2.cloned.1.call-done = bf16[128,4096]{1,0:T(8,128)(2,1)} async-done(((bf16[128,4096]{1,0:T(8,128)(2,1)}), bf16[128,4096]{1,0:T(8,128)(2,1)}) %all-reduce.2.cloned.1.call-update) | async-done | bytes 1048592 | tf_op jit(solution)/shard_map/psum | solution.py:102
  380.4 1.7 multiply_reduce_fusion
  382.1 57.7 %all-gather.11.cloned.1.call-done = bf16[4096,512]{1,0:T(8,128)(2,1)} async-done(((bf16[1024,512]{1,0:T(8,128)(2,1)}), bf16[4096,512]{1,0:T(8,128)(2,1)}) %all-gather.11.cloned.1.call-update) | async-done | bytes 4194320 | tf_op jit(solution)/shard_map/all_gather | solution.py:110
  439.9 2.9 convolution_convert_fusion.1
  442.9 32.6 %while.31 = (s32[]{:T(128)}, f32[1,4,128]{2,1,0:T(4,128)S(1)}, f32[1,4,128]{2,1,0:T(4,128)S(1)}, f32[1,4,128,128]{3,2,1,0:T(8,128)S(1)}, s32[16,512]{1,0:T(8,128...) while((s32[]{:T(128)}, f32[1,4,128]{2,1,0:T(4,128)S(1)}, ...), condition=%wide.region_9.10_spmd.clone, body=%wide.region_6.9_spmd.clone.sunk | while | flops 136317952 | bytes 4758137 | solution.py:67
  442.9 1.0 dynamic-slice_bitcast_fusion.5
  449.0 1.0 dynamic-slice_bitcast_fusion.5
  457.2 1.0 dynamic-slice_bitcast_fusion.5
  463.3 1.0 dynamic-slice_bitcast_fusion.5
  471.4 1.0 dynamic-slice_bitcast_fusion.5
  476.4 1.5 convert_add_fusion
  (312 shorter events, 51.6 us)
Async XLA Ops:
  7.2 45.5 %all-gather.5.cloned.1.call-start = ((), (), s32[]{:S(2)}) async-start(), calls=%async_computation | async-start | bytes 2621440 | tf_op jit(solution)/shard_map/all_gather | solution.py:83
  7.9 213.5 %all-gather.7.cloned.1.call-start = ((), (), s32[]{:S(2)}) async-start(), calls=%async_computation.1 | async-start | bytes 4259840 | tf_op jit(solution)/shard_map/all_gather | solution.py:91
  8.6 48.2 %copy-start.3 = (s32[8192]{0:T(1024)S(1)}, s32[8192]{0:T(1024)}, u32[]{:S(2)}) copy-start(s32[8192]{0:T(1024)} %param.15) | copy-start | bytes 98308
  8.6 48.3 %copy-start.2 = (bf16[128,512]{1,0:T(8,128)(2,1)S(1)}, bf16[128,512]{1,0:T(8,128)(2,1)}, u32[]{:S(2)}) copy-start(bf16[128,512]{1,0:T(8,128)(2,1)} %param.16) | copy-start | bytes 393220
  56.0 220.5 %all-gather.9.cloned.1.call-start = ((), (), s32[]{:S(2)}) async-start(), calls=%async_computation.2 | async-start | bytes 5242880 | tf_op jit(solution)/shard_map/all_gather | solution.py:97
  56.7 323.7 %all-reduce.2.cloned.1.call-start = ((), (), s32[]{:S(2)}) async-start(), calls=%async_computation.3 | async-start | bytes 2097152 | tf_op jit(solution)/shard_map/psum | solution.py:102
  280.4 0.7 copy-start.4
  280.4 100.0 %copy-start = (bf16[128,4096]{1,0:T(8,128)(2,1)S(1)}, bf16[128,4096]{1,0:T(8,128)(2,1)}, u32[]{:S(2)}) copy-start(bf16[128,4096]{1,0:T(8,128)(2,1)} %param.12) | copy-start | bytes 3145732
  280.4 159.4 %all-gather.11.cloned.1.call-start = ((), (), s32[]{:S(2)}) async-start(), calls=%async_computation.4 | async-start | bytes 5242880 | tf_op jit(solution)/shard_map/all_gather | solution.py:110
  380.4 59.5 %copy-start.1 = (bf16[128,4096]{1,0:T(8,128)(2,1)S(1)}, bf16[128,4096]{1,0:T(8,128)(2,1)}, u32[]{:S(2)}) copy-start(bf16[128,4096]{1,0:T(8,128)(2,1)} %all-reduce.2.cloned.1.call-done) | copy-start | bytes 3145732
Sparse Core Ops, SparseCore 0:
  10.1 42.5 all-gather.4
  56.1 165.2 all-gather.6
  223.5 52.9 all-gather.8
  280.6 99.7 all-reduce.1
  382.3 57.4 all-gather.10
where the time goes:
time: 487 us; the launch traced here: 485 us
  waiting for transfers between devices  376 us (77%)
  local copies, waits for them, and re-layouts  47.6 us (10%)
  matrix products  31.4 us (6%)
  other arithmetic  14.3 us (3%)
  between operations  14 us (3%)
    all_gather x1, waiting for transfers between devices, per_device(): lax.all_gather(cache_local, ('section', 'ctx'), axis=0, tiled=True)  164 us
    psum x1, waiting for transfers between devices, per_device(): lax.psum(partial_value.astype(jnp.bfloat16), 'head').astype(jnp.float32)  99.3 us
    all_gather x1, waiting for transfers between devices, per_device(): lax.all_gather(query_weight, 'section', axis=0, tiled=True)  57.7 us
    all_gather x1, waiting for transfers between devices, per_device(): lax.all_gather(kv_weight, 'section', axis=0, tiled=True)  44 us
    squeeze x32, local copies, waits for them, and re-layouts, attend(): lax.scan(absorb, (start_high, start_denominator, start_accumulated), (cac...  31.2 us
    unnamed x16, local copies, waits for them, and re-layouts  14.9 us
    dot_general x32, matrix products, absorb(): jnp.einsum('kgts,skd->kgtd', weights.astype(jnp.bfloat16), cache_block[:,...  11.3 us
    dot_general x32, matrix products, absorb(): jnp.einsum('tkgd,skd->kgts', query_heads, cache_block[:, :, 0, :], prefer...  9.92 us
  transfers between devices with their start and end apart: 5, of which 5 were waited for; matrix products, arithmetic and copies ran while one was open for 10% of the time, Pallas kernels for 0%

commit v1 on v0

v1 whole, which is shorter than its diff:
```python
import functools
import math

import jax
import jax.numpy as jnp
from jax import lax
from jax.experimental import pallas as pl
from jax.experimental.pallas import tpu as pltpu
from jax.sharding import PartitionSpec as P

HD = 128
KV = 2 * HD
TAIL = 16
VMEM_LIMIT = 48 * 2**20

SMEM_SPEC = pl.BlockSpec(memory_space=pltpu.SMEM)
VMEM_SPEC = pl.BlockSpec(memory_space=pltpu.VMEM)


def dot(a, b):
    return jnp.dot(a, b, preferred_element_type=jnp.float32)


def kv_partial_kernel(section, hidden, from_near, from_far, weight, mate_weight, own, near):
    depth = weight.shape[0]
    here = section[0]
    mine = hidden[:, pl.ds(pl.multiple_of(here * depth, depth), depth)]
    mates = hidden[:, pl.ds(pl.multiple_of((here ^ 1) * depth, depth), depth)]
    rows = mine.shape[0]
    both = dot(jnp.concatenate([mine, from_near[...]], axis=0), weight[...]) + dot(
        jnp.concatenate([mates, from_far[...]], axis=0), mate_weight[...]
    )
    own[...] = both[:rows]
    near[...] = both[rows:].astype(jnp.bfloat16)


def kv_partial(section, hidden, from_near, from_far, weight, mate_weight):
    shape = (hidden.shape[0], weight.shape[1])
    return pl.pallas_call(
        kv_partial_kernel,
        out_shape=(
            jax.ShapeDtypeStruct(shape, jnp.float32),
            jax.ShapeDtypeStruct(shape, jnp.bfloat16),
        ),
        in_specs=[SMEM_SPEC] + [VMEM_SPEC] * 5,
        out_specs=(VMEM_SPEC, VMEM_SPEC),
        compiler_params=pltpu.CompilerParams(vmem_limit_bytes=VMEM_LIMIT),
        name="kv_partial",
    )(section, hidden, from_near, from_far, weight, mate_weight)


def rotate_kernel(signs, own, other, head, tail):
    row = lax.broadcasted_iota(jnp.int32, (HD, HD), 0)
    column = lax.broadcasted_iota(jnp.int32, (HD, HD), 1)
    meet = row & column
    parity = meet ^ (meet >> 4)
    parity = parity ^ (parity >> 2)
    parity = (parity ^ (parity >> 1)) & 1
    table = (1 - 2 * parity).astype(jnp.float32).astype(jnp.bfloat16)
    sign = signs[...].astype(jnp.float32)
    split = head.shape[0]
    for c in range(2):
        columns = slice(c * HD, (c + 1) * HD)
        value = (own[:, columns] + other[:, columns].astype(jnp.float32)) * sign
        top = value.astype(jnp.bfloat16)
        value = value - top.astype(jnp.float32)
        middle = value.astype(jnp.bfloat16)
        low = (value - middle.astype(jnp.float32)).astype(jnp.bfloat16)
        rotated = (dot(low, table) + dot(middle, table)) + dot(top, table)
        rotated = (rotated * jnp.float32(1.0 / math.sqrt(HD))).astype(jnp.bfloat16)
        head[:, columns] = rotated[:split]
        tail[:, columns] = rotated[split:]


def rotate(signs, own, other):
    rows = own.shape[0]
    return pl.pallas_call(
        rotate_kernel,
        out_shape=(
            jax.ShapeDtypeStruct((rows - TAIL, KV), jnp.bfloat16),
            jax.ShapeDtypeStruct((TAIL, KV), jnp.bfloat16),
        ),
        in_specs=[VMEM_SPEC] * 3,
        out_specs=(VMEM_SPEC, VMEM_SPEC),
        name="rotate",
    )(signs, own, other)


def attend_kernel(place, query, body_pos, tail_pos, *refs):
    bodies, tail, out = refs[:-2], refs[-2], refs[-1]
    rows = query.shape[0]
    group = query.shape[1] // HD
    scale = jnp.float32(math.log2(math.e) / math.sqrt(HD))
    section, first = place[0], place[1]
    parts = [(ref, body_pos, section ^ j) for j, ref in enumerate(bodies)]
    parts.append((tail, tail_pos, 0))
    q = jnp.concatenate([query[:, g * HD : (g + 1) * HD] for g in range(group)], axis=0)
    highest = jnp.full((group * rows, 1), -1e30, jnp.float32)
    total = jnp.zeros((group * rows, 2 * HD), jnp.float32)
    for ref, pos, index in parts:
        size = ref.shape[0]
        scores = lax.dot_general(
            q, ref[:, :HD], (((1,), (1,)), ((), ())), preferred_element_type=jnp.float32
        )
        query_pos = first + lax.broadcasted_iota(jnp.int32, (rows, size), 0)
        allowed = pos[pl.ds(index, 1), :] <= query_pos
        scores = jnp.where(allowed[None], scores.reshape(group, rows, size), -jnp.inf)
        scores = scores.reshape(group * rows, size)
        new_high = jnp.maximum(highest, jnp.max(scores, axis=1, keepdims=True))
        weights = jnp.exp2((scores - new_high) * scale).astype(jnp.bfloat16)
        shrink = jnp.exp2((highest - new_high) * scale)
        value = ref[:, HD:]
        value = jnp.concatenate([value, jnp.ones_like(value)], axis=1)
        total = total * shrink + dot(weights, value)
        highest = new_high
    attended = (total[:, :HD] / total[:, HD:]).astype(jnp.bfloat16)
    for g in range(group):
        out[:, g * HD : (g + 1) * HD] = attended[g * rows : (g + 1) * rows]


def attend(place, query, body_pos, tail_pos, bodies, tail):
    return pl.pallas_call(
        attend_kernel,
        out_shape=jax.ShapeDtypeStruct(query.shape, jnp.bfloat16),
        in_specs=[SMEM_SPEC] + [VMEM_SPEC] * (4 + len(bodies)),
        out_specs=VMEM_SPEC,
        compiler_params=pltpu.CompilerParams(vmem_limit_bytes=VMEM_LIMIT),
        name="attend",
    )(place, query, body_pos, tail_pos, *bodies, tail)


def out_kernel(first, weight, out):
    out[0] = dot(first[...], weight[0]).astype(jnp.bfloat16)


def out_project(first, weight, heads):
    sections, depth, width = weight.shape
    each = heads // sections
    share = width // each
    rows = first.shape[0]
    return pl.pallas_call(
        out_kernel,
        grid=(heads,),
        out_shape=jax.ShapeDtypeStruct((heads, rows, share), jnp.bfloat16),
        in_specs=[
            pl.BlockSpec((rows, depth), lambda h: (0, 0)),
            pl.BlockSpec((1, depth, share), lambda h: (h // each, 0, h % each)),
        ],
        out_specs=pl.BlockSpec((1, rows, share), lambda h: (h, 0, 0)),
        name="out_project",
    )(first, weight)


def query_kernel(width, scaled, inverse, weight, out, total, square):
    step = pl.program_id(0)

    @pl.when(step == 0)
    def _():
        total[...] = jnp.zeros_like(total)
        square[...] = jnp.zeros_like(square)

    block = scaled[0]
    total[...] += dot(block, weight[...])
    plain = block.astype(jnp.float32) * inverse[0]
    square[...] += jnp.sum(plain * plain, axis=1, keepdims=True)

    @pl.when(step == pl.num_programs(0) - 1)
    def _():
        root = lax.rsqrt(square[...] / width + 1e-6)
        out[...] = (total[...] * root).astype(jnp.bfloat16)


def query_project(scaled, inverse, weight):
    heads, rows, share = scaled.shape
    width = weight.shape[1]
    return pl.pallas_call(
        functools.partial(query_kernel, heads * share),
        grid=(heads,),
        out_shape=jax.ShapeDtypeStruct((rows, width), jnp.bfloat16),
        in_specs=[
            pl.BlockSpec((1, rows, share), lambda h: (h, 0, 0)),
            pl.BlockSpec((1, 1, share), lambda h: (h, 0, 0)),
            pl.BlockSpec((share, width), lambda h: (h, 0)),
        ],
        out_specs=pl.BlockSpec((rows, width), lambda h: (0, 0)),
        scratch_shapes=[
            pltpu.VMEM((rows, width), jnp.float32),
            pltpu.VMEM((rows, 1), jnp.float32),
        ],
        name="query_project",
    )(scaled, inverse, weight)


def per_device(
    self_hidden, kv_weight, signs, positions, queries, out_weight, query_weight, norm_gain
):
    rows, width = self_hidden.shape
    sections, ctxs, heads = (lax.axis_size(a) for a in ("section", "ctx", "head"))
    section, ctx, head = (lax.axis_index(a) for a in ("section", "ctx", "head"))
    share = width // heads
    depth = width // sections

    def swap_core(value):
        return lax.ppermute(value, "section", [(i, i ^ 1) for i in range(sections)])

    def swap_y(value):
        return lax.ppermute(value, "section", [(i, i ^ 2) for i in range(sections)])

    def swap_far_y(value):
        pairs = [
            (s * heads + h, (s ^ 2) * heads + (h ^ 1))
            for s in range(sections)
            for h in range(heads)
        ]
        return lax.ppermute(value, ("section", "head"), pairs)

    out_all = lax.all_gather(out_weight, "section", axis=0)
    query_all = lax.all_gather(query_weight, "section", axis=0, tiled=True)

    body = rows - TAIL
    pos = positions.reshape(sections, ctxs, rows)
    body_pos = pos[:, :, :body].reshape(sections, ctxs * body)
    tail_pos = jnp.transpose(pos[:, :, body:], (1, 0, 2)).reshape(1, ctxs * sections * TAIL)
    first_pos = lax.dynamic_index_in_dim(positions, (section * ctxs + ctx) * rows, 0, False)
    place = jnp.stack([section, first_pos])

    def columns(of):
        return lax.dynamic_slice_in_dim(self_hidden, of * depth, depth, 1)

    from_near = swap_y(columns(section ^ 2))
    from_far = swap_far_y(columns(section ^ 3))
    mate_weight = swap_core(kv_weight)
    own, near = kv_partial(place, self_hidden, from_near, from_far, kv_weight, mate_weight)
    cache_body, cache_tail = rotate(signs, own, swap_y(near))

    cache_tail = lax.all_gather(cache_tail, "section", axis=0, tiled=True)
    body_own = lax.all_gather(cache_body, "ctx", axis=0, tiled=True)
    body_near = swap_y(body_own)
    body_mate = swap_core(body_own)
    tail = lax.all_gather(cache_tail, "ctx", axis=0, tiled=True)
    body_last = swap_core(body_near)
    bodies = (body_own, body_mate, body_near, body_last)

    first = attend(place, queries, body_pos, tail_pos, bodies, tail)
    partial = out_project(first, out_all, heads)
    pieces = lax.all_to_all(partial, "head", 0, 0, tiled=True)
    own_hidden = lax.dynamic_slice_in_dim(self_hidden, head * share, share, 1)
    residual = own_hidden.astype(jnp.float32) + jnp.sum(pieces.astype(jnp.float32), axis=0)
    gain = norm_gain.astype(jnp.float32)
    own_gain = lax.dynamic_slice_in_dim(gain, head * share, share, 0)
    scaled = (residual * own_gain).astype(jnp.bfloat16)
    spread = jnp.broadcast_to(scaled[None], (heads, rows, share))
    scaled_all = lax.all_to_all(spread, "head", 0, 0, tiled=True)
    inverse = (1.0 / gain).reshape(heads, 1, share)
    second_queries = query_project(scaled_all, inverse, query_all)
    second = attend(place, second_queries, body_pos, tail_pos, bodies, tail)
    return (residual.astype(jnp.bfloat16), second)


def solution(mesh):
    return jax.shard_map(
        per_device,
        mesh=mesh,
        in_specs=(
            P(("section", "ctx"), None),
            P("section", "head"),
            P("head", None),
            P(),
            P(("section", "ctx"), "head"),
            P("head", "section"),
            P("section", "head"),
            P(),
        ),
        out_specs=(P(("section", "ctx"), "head"), P(("section", "ctx"), "head")),
        check_vma=False,
    )
```

time: 487 us -> 220 us (0.45)
  the two profiles are of different devices: /device:TPU:1 before, /device:TPU:32 now
where the time goes in v1:
time: 220 us; the launch traced here: 219 us
  blocking collectives  80.2 us (36%)
  waiting for transfers between devices  53.1 us (24%)
  Pallas kernels  30.1 us (14%)
  starting transfers between devices  27.9 us (13%)
  between operations  14.2 us (6%)
  local copies, waits for them, and re-layouts  8.88 us (4%)
  other arithmetic  4.32 us (2%)
    all_gather x1, blocking collectives, per_device(): body_own = lax.all_gather(cache_body, 'ctx', axis=0, tiled=True)  39.4 us
    all_gather x1, blocking collectives, per_device(): tail = lax.all_gather(cache_tail, 'ctx', axis=0, tiled=True)  35.3 us
    ppermute x3, waiting for transfers between devices, swap_y(): return lax.ppermute(value, 'section', [(i, i ^ 2) for i in range(sections)])  24.1 us
    pallas_call x2, Pallas kernels, attend(): pl.pallas_call(attend_kernel, out_shape=jax.ShapeDtypeStruct(query.shape,...  14.1 us
    all_to_all x1, waiting for transfers between devices, per_device(): pieces = lax.all_to_all(partial, 'head', 0, 0, tiled=True)  12 us
    all_to_all x1, waiting for transfers between devices, per_device(): scaled_all = lax.all_to_all(spread, 'head', 0, 0, tiled=True)  11.2 us
    ppermute x3, starting transfers between devices, swap_y(): return lax.ppermute(value, 'section', [(i, i ^ 2) for i in range(sections)])  7.3 us
    pallas_call x1, Pallas kernels, out_project(): pl.pallas_call(out_kernel, grid=(heads,), out_shape=jax.ShapeDtypeStruct(...  6.67 us
  transfers between devices with their start and end apart: 11, of which 6 were waited for; matrix products, arithmetic and copies ran while one was open for 4% of the time, Pallas kernels for 7%

profile of v1, /device:TPU:32, one launch (start us, length us, event | category | flops | bytes accessed | tf_op | source)
XLA Modules:
  0.0 218.8 jit_solution(7842846000881143628)
XLA Ops:
  8.7 1.9 collective-permute-start.2
  10.6 1.1 constant_dynamic-slice_fusion
  11.7 3.5 %collective-permute-start = (bf16[128,1024]{1,0:T(8,128)(2,1)S(1)}, bf16[128,1024]{1,0:T(8,128)(2,1)S(1)}, u32[]{:S(2)}, u32[]{:S(2)}) collective-permute-start(bf16[128,1024]{1,0:T(8,128)(2,1)S(1)} %get-tuple-element.13), channel_id=1, source_target_pairs={{0,256},{128,384},{256,0},{384,128},{1,257},{129,385},{257,1},{385... | collective-permute-start | bytes 786440 | tf_op jit(solution)/shard_map/ppermute | solution.py:207
  15.2 4.1 %collective-permute-start.1 = (bf16[128,1024]{1,0:T(8,128)(2,1)S(1)}, bf16[128,1024]{1,0:T(8,128)(2,1)S(1)}, u32[]{:S(2)}, u32[]{:S(2)}) collective-permute-start(bf16[128,1024]{1,0:T(8,128)(2,1)S(1)} %get-tuple-element.12), channel_id=1, source_target_pairs={{0,257},{1,256},{2,259},{3,258},{4,261},{5,260},{6,263},{7,262},{1... | collective-permute-start | bytes 786440 | tf_op jit(solution)/shard_map/ppermute | solution.py:215
  19.3 1.3 dynamic_slice.17
  21.3 1.0 collective-permute-done.from_near
  22.3 4.4 %collective-permute-done.1.from_far = bf16[128,1024]{1,0:T(8,128)(2,1)S(1)} collective-permute-done((bf16[128,1024]{1,0:T(8,128)(2,1)S(1)}, bf16[128,1024]{1,0:T(8,128)(2,1)S(1)}, u32[]{:S(2)}, u32[]{:S(2)}) %collective-permute-start.1) | collective-permute-done | bytes 262176 | tf_op jit(solution)/shard_map/ppermute | solution.py:215
  26.7 1.2 copy-done
  27.9 1.0 copy-done.1
  29.0 1.0 kv_partial.1
  30.7 1.9 collective-permute-start.3
  32.6 5.3 %collective-permute-done.3.other = bf16[128,256]{1,0:T(8,128)(2,1)S(1)} collective-permute-done((bf16[128,256]{1,0:T(8,128)(2,1)S(1)}, bf16[128,256]{1,0:T(8,128)(2,1)S(1)}, u32[]{:S(2)}, u32[]{:S(2)}) %collective-permute-start.3) | collective-permute-done | bytes 65568 | tf_op jit(solution)/shard_map/ppermute | solution.py:207
  38.5 1.8 rotate.1
  40.3 39.4 %all_gather.18.refs_0_ = bf16[1792,256]{1,0:T(8,128)(2,1)S(1)} all-gather(bf16[112,256]{1,0:T(8,128)(2,1)} %get-tuple-element.8), channel_id=1, replica_groups=mesh['section'=4,'ctx'=16,'head'=8] {'ctx'}, dimensions={0}, use_global_device_ids=true | all-gather | bytes 974848 | tf_op jit(solution)/shard_map/all_gather | solution.py:237
  79.8 1.9 collective-permute-start.5
  81.7 1.9 collective-permute-start.4
  83.6 17.7 %collective-permute-done.5.refs_2_ = bf16[1792,256]{1,0:T(8,128)(2,1)S(1)} collective-permute-done((bf16[1792,256]{1,0:T(8,128)(2,1)S(1)}, bf16[1792,256]{1,0:T(8,128)(2,1)S(1)}, u32[]{:S(2)}, u32[]{:S(2)}) %collective-permute-start.5) | collective-permute-done | bytes 917536 | tf_op jit(solution)/shard_map/ppermute | solution.py:207
  101.3 1.9 collective-permute-start.6
  103.5 5.5 %all_gather.19 = bf16[64,256]{1,0:T(8,128)(2,1)S(1)} all-gather(bf16[16,256]{1,0:T(8,128)(2,1)} %get-tuple-element.9), channel_id=1, replica_groups=mesh['section'=4,'ctx'=16,'head'=8] {'section'}, dimensions={0}, use_global_device_ids=true | all-gather | bytes 40960 | tf_op jit(solution)/shard_map/all_gather | solution.py:236
  109.1 35.3 %all_gather.20.refs_4_ = bf16[1024,256]{1,0:T(8,128)(2,1)S(1)} all-gather(bf16[64,256]{1,0:T(8,128)(2,1)S(1)} %all_gather.19), channel_id=1, replica_groups=mesh['section'=4,'ctx'=16,'head'=8] {'ctx'}, dimensions={0}, use_global_device_ids=true | all-gather | bytes 557056 | tf_op jit(solution)/shard_map/all_gather | solution.py:240
  144.4 6.7 %attend.2.first = bf16[128,512]{1,0:T(8,128)(2,1)S(1)} custom-call(s32[2]{0:T(128)S(1)} %pad_add_fusion.section.place, bf16[128,512]{1,0:T(8,128)(2,1)S(1)} %copy-done.4, s32[4,1792]{1,0:T(4,128)S(1)} %reshape.19.body_pos, s32[1,1024]{1,0:T(1,128)S(1)} %reshape.20.tail_pos, bf16[1792,256]{1,0:T(8,128)(2,1)S(1)} %all_gather.18.refs_0_, ...), custom_call_target="tpu_custom_call" | custom-call | tf_op jit(solution)/shard_map/attend/pallas_call | solution.py:122
  151.8 6.7 %out_project.1 = bf16[8,128,512]{2,1,0:T(8,128)(2,1)} custom-call(bf16[128,512]{1,0:T(8,128)(2,1)} %copy-done.3, bf16[4,512,1024]{2,1,0:T(8,128)(2,1)} %bitcast.7), custom_call_target="tpu_custom_call" | custom-call | tf_op jit(solution)/shard_map/out_project/pallas_call | solution.py:141
  158.4 6.3 %all-to-all-start = ((bf16[8,128,512]{2,1,0:T(8,128)(2,1)}), bf16[8,128,512]{2,1,0:T(8,128)(2,1)}, u32[]{:S(2)}, u32[]{:S(2)}) async-start(bf16[8,128,512]{2,1,0:T(8,128)(2,1)} %out_project.1), calls=%async_computation | async-start | bytes 2097152 | tf_op jit(solution)/shard_map/all_to_all | solution.py:246
  164.8 12.0 %all-to-all-done = bf16[8,128,512]{2,1,0:T(8,128)(2,1)} async-done(((bf16[8,128,512]{2,1,0:T(8,128)(2,1)}), bf16[8,128,512]{2,1,0:T(8,128)(2,1)}, u32[]{:S(2)}, u32[]{:S(2)}) %all-to-all-start) | async-done | bytes 1048608 | tf_op jit(solution)/shard_map/all_to_all | solution.py:246
  176.8 1.4 convert_reduce_fusion
  178.2 1.6 multiply_convert_fusion
  179.8 1.1 broadcast_in_dim.2
  180.9 4.4 %all-to-all-start.1 = ((bf16[8,128,512]{2,1,0:T(8,128)(2,1)}), bf16[8,128,512]{2,1,0:T(8,128)(2,1)}, u32[]{:S(2)}, u32[]{:S(2)}) async-start(bf16[8,128,512]{2,1,0:T(8,128)(2,1)} %broadcast_in_dim.2), calls=%async_computation.1 | async-start | bytes 2097152 | tf_op jit(solution)/shard_map/all_to_all | solution.py:253
  185.9 11.2 %all-to-all-done.1.scaled = bf16[8,128,512]{2,1,0:T(8,128)(2,1)} async-done(((bf16[8,128,512]{2,1,0:T(8,128)(2,1)}), bf16[8,128,512]{2,1,0:T(8,128)(2,1)}, u32[]{:S(2)}, u32[]{:S(2)}) %all-to-all-start.1) | async-done | bytes 1048608 | tf_op jit(solution)/shard_map/all_to_all | solution.py:253
  197.1 6.5 %query_project.1.query = bf16[128,512]{1,0:T(8,128)(2,1)} custom-call(bf16[8,128,512]{2,1,0:T(8,128)(2,1)} %all-to-all-done.1.scaled, f32[8,1,512]{2,1,0:T(1,128)} %bitcast.10, bf16[4096,512]{1,0:T(8,128)(2,1)} %all-gather.4.cloned.1.call-done.weight), custom_call_target="tpu_custom_call" | custom-call | tf_op jit(solution)/shard_map/query_project/pallas_call | solution.py:176
  203.7 0.9 copy-done.2
  204.6 7.4 %attend.3 = bf16[128,512]{1,0:T(8,128)(2,1)} custom-call(s32[2]{0:T(128)S(1)} %pad_add_fusion.section.place, bf16[128,512]{1,0:T(8,128)(2,1)S(1)} %copy-done.2, s32[4,1792]{1,0:T(4,128)S(1)} %reshape.19.body_pos, s32[1,1024]{1,0:T(1,128)S(1)} %reshape.20.tail_pos, bf16[1792,256]{1,0:T(8,128)(2,1)S(1)} %all_gather.18.refs_0_, ...), custom_call_target="tpu_custom_call" | custom-call | tf_op jit(solution)/shard_map/attend/pallas_call | solution.py:122
  (31 shorter events, 5.1 us)
Async XLA Ops:
  7.2 96.1 %copy-start.6 = (s32[8192]{0:T(1024)S(1)}, s32[8192]{0:T(1024)}, u32[]{:S(2)}) copy-start(s32[8192]{0:T(1024)} %param.11) | copy-start | bytes 98308
  7.2 137.2 %copy-start.4 = (bf16[128,512]{1,0:T(8,128)(2,1)S(1)}, bf16[128,512]{1,0:T(8,128)(2,1)}, u32[]{:S(2)}) copy-start(bf16[128,512]{1,0:T(8,128)(2,1)} %query.1) | copy-start | bytes 393220
  7.2 144.6 %all-gather.6.cloned.1.call-start = ((), (), s32[]{:S(2)}) async-start(), calls=%async_computation.3 | async-start | bytes 5242880 | tf_op jit(solution)/shard_map/all_gather | solution.py:217
  7.9 178.0 %all-gather.4.cloned.1.call-start = ((), (), s32[]{:S(2)}) async-start(), calls=%async_computation.2 | async-start | bytes 5242880 | tf_op jit(solution)/shard_map/all_gather | solution.py:218
  8.7 18.1 %collective-permute-start.2 = (bf16[1024,256]{1,0:T(8,128)(2,1)}, bf16[1024,256]{1,0:T(8,128)(2,1)S(1)}, u32[]{:S(2)}, u32[]{:S(2)}) collective-permute-start(bf16[1024,256]{1,0:T(8,128)(2,1)} %weight.1), channel_id=1, source_target_pairs={{0,128},{128,0},{256,384},{384,256},{1,129},{129,1},{257,385},{385... | collective-permute-start | bytes 1572872 | tf_op jit(solution)/shard_map/ppermute | solution.py:204
  11.7 10.6 %collective-permute-start = (bf16[128,1024]{1,0:T(8,128)(2,1)S(1)}, bf16[128,1024]{1,0:T(8,128)(2,1)S(1)}, u32[]{:S(2)}, u32[]{:S(2)}) collective-permute-start(bf16[128,1024]{1,0:T(8,128)(2,1)S(1)} %get-tuple-element.13), channel_id=1, source_target_pairs={{0,256},{128,384},{256,0},{384,128},{1,257},{129,385},{257,1},{385... | collective-permute-start | bytes 786440 | tf_op jit(solution)/shard_map/ppermute | solution.py:207
  15.2 11.5 %collective-permute-start.1 = (bf16[128,1024]{1,0:T(8,128)(2,1)S(1)}, bf16[128,1024]{1,0:T(8,128)(2,1)S(1)}, u32[]{:S(2)}, u32[]{:S(2)}) collective-permute-start(bf16[128,1024]{1,0:T(8,128)(2,1)S(1)} %get-tuple-element.12), channel_id=1, source_target_pairs={{0,257},{1,256},{2,259},{3,258},{4,261},{5,260},{6,263},{7,262},{1... | collective-permute-start | bytes 786440 | tf_op jit(solution)/shard_map/ppermute | solution.py:215
  26.7 1.2 copy-start
  27.9 1.0 copy-start.1
  30.0 0.7 copy-start.5
  30.7 7.3 %collective-permute-start.3 = (bf16[128,256]{1,0:T(8,128)(2,1)S(1)}, bf16[128,256]{1,0:T(8,128)(2,1)S(1)}, u32[]{:S(2)}, u32[]{:S(2)}) collective-permute-start(bf16[128,256]{1,0:T(8,128)(2,1)S(1)} %get-tuple-element.7), channel_id=1, source_target_pairs={{0,256},{128,384},{256,0},{384,128},{1,257},{129,385},{257,1},{385... | collective-permute-start | bytes 196616 | tf_op jit(solution)/shard_map/ppermute | solution.py:207
  37.9 0.6 copy-start.7
  79.8 21.5 %collective-permute-start.5 = (bf16[1792,256]{1,0:T(8,128)(2,1)S(1)}, bf16[1792,256]{1,0:T(8,128)(2,1)S(1)}, u32[]{:S(2)}, u32[]{:S(2)}) collective-permute-start(bf16[1792,256]{1,0:T(8,128)(2,1)S(1)} %all_gather.18.refs_0_), channel_id=1, source_target_pairs={{0,256},{128,384},{256,0},{384,128},{1,257},{129,385},{257,1},{385... | collective-permute-start | bytes 2752520 | tf_op jit(solution)/shard_map/ppermute | solution.py:207
  81.7 62.7 %collective-permute-start.4 = (bf16[1792,256]{1,0:T(8,128)(2,1)S(1)}, bf16[1792,256]{1,0:T(8,128)(2,1)S(1)}, u32[]{:S(2)}, u32[]{:S(2)}) collective-permute-start(bf16[1792,256]{1,0:T(8,128)(2,1)S(1)} %all_gather.18.refs_0_), channel_id=1, source_target_pairs={{0,128},{128,0},{256,384},{384,256},{1,129},{129,1},{257,385},{385... | collective-permute-start | bytes 2752520 | tf_op jit(solution)/shard_map/ppermute | solution.py:204
  101.3 43.0 %collective-permute-start.6 = (bf16[1792,256]{1,0:T(8,128)(2,1)S(1)}, bf16[1792,256]{1,0:T(8,128)(2,1)}, u32[]{:S(2)}, u32[]{:S(2)}) collective-permute-start(bf16[1792,256]{1,0:T(8,128)(2,1)S(1)} %collective-permute-done.5.refs_2_), channel_id=1, source_target_pairs={{0,128},{128,0},{256,384},{384,256},{1,129},{129,1},{257,385},{385... | collective-permute-start | bytes 2752520 | tf_op jit(solution)/shard_map/ppermute | solution.py:204
  151.1 0.7 copy-start.3
  151.8 13.0 %copy-start.8 = (bf16[4096]{0:T(1024)(128)(2,1)S(1)}, bf16[4096]{0:T(1024)(128)(2,1)}, u32[]{:S(2)}) copy-start(bf16[4096]{0:T(1024)(128)(2,1)} %param.15) | copy-start | bytes 24580
  158.4 18.4 %all-to-all-start = ((bf16[8,128,512]{2,1,0:T(8,128)(2,1)}), bf16[8,128,512]{2,1,0:T(8,128)(2,1)}, u32[]{:S(2)}, u32[]{:S(2)}) async-start(bf16[8,128,512]{2,1,0:T(8,128)(2,1)} %out_project.1), calls=%async_computation | async-start | bytes 2097152 | tf_op jit(solution)/shard_map/all_to_all | solution.py:246
  180.9 16.2 %all-to-all-start.1 = ((bf16[8,128,512]{2,1,0:T(8,128)(2,1)}), bf16[8,128,512]{2,1,0:T(8,128)(2,1)}, u32[]{:S(2)}, u32[]{:S(2)}) async-start(bf16[8,128,512]{2,1,0:T(8,128)(2,1)} %broadcast_in_dim.2), calls=%async_computation.1 | async-start | bytes 2097152 | tf_op jit(solution)/shard_map/all_to_all | solution.py:253
  203.7 0.9 copy-start.2
Sparse Core Ops, SparseCore 0:
  10.1 59.1 all-gather.5
  71.5 58.6 all-gather.3

commit v2 on v1

v2 whole, which is shorter than its diff:
```python
import math

import jax
import jax.numpy as jnp
from jax import lax
from jax.experimental import pallas as pl
from jax.experimental.pallas import tpu as pltpu
from jax.sharding import PartitionSpec as P

HD = 128
KV = 2 * HD
SCALE_ROWS = 16
TOP = 13.0
SCORE_SCALE = math.log2(math.e) / math.sqrt(HD)
LIMITS = pltpu.CompilerParams(vmem_limit_bytes=48 * 2**20)

SMEM_SPEC = pl.BlockSpec(memory_space=pltpu.SMEM)
VMEM_SPEC = pl.BlockSpec(memory_space=pltpu.VMEM)


def dot(a, b):
    return jnp.dot(a, b, preferred_element_type=jnp.float32)


def kv_partial_kernel(place, hidden, from_near, from_far, weight, mate_weight, out, send):
    depth = weight.shape[0]
    section = place[0]
    mine = hidden[:, pl.ds(pl.multiple_of(section * depth, depth), depth)]
    mates = hidden[:, pl.ds(pl.multiple_of((section ^ 1) * depth, depth), depth)]
    both = dot(jnp.concatenate([mine, from_near[...]], axis=0), weight[...]) + dot(
        jnp.concatenate([mates, from_far[...]], axis=0), mate_weight[...]
    )
    out[...] = both
    send[...] = both.astype(jnp.bfloat16)


def kv_partial(place, hidden, from_near, from_far, weight, mate_weight):
    shape = (2 * hidden.shape[0], weight.shape[1])
    return pl.pallas_call(
        kv_partial_kernel,
        out_shape=(
            jax.ShapeDtypeStruct(shape, jnp.float32),
            jax.ShapeDtypeStruct(shape, jnp.bfloat16),
        ),
        in_specs=[SMEM_SPEC] + [VMEM_SPEC] * 5,
        out_specs=(VMEM_SPEC, VMEM_SPEC),
        compiler_params=LIMITS,
        name="kv_partial",
    )(place, hidden, from_near, from_far, weight, mate_weight)


def rotate_kernel(place, signs, own, other, out):
    row = lax.broadcasted_iota(jnp.int32, (HD, HD), 0)
    column = lax.broadcasted_iota(jnp.int32, (HD, HD), 1)
    meet = row & column
    parity = meet ^ (meet >> 4)
    parity = parity ^ (parity >> 2)
    parity = (parity ^ (parity >> 1)) & 1
    table = (1 - 2 * parity).astype(jnp.float32).astype(jnp.bfloat16)
    sign = signs[...].astype(jnp.float32)
    rows = own.shape[0] // 2
    side = place[0] >> 1
    for c in range(2):
        columns = slice(c * HD, (c + 1) * HD)
        theirs = other[:, columns].astype(jnp.float32)
        value = own[:, columns] + jnp.concatenate([theirs[rows:], theirs[:rows]], axis=0)
        value = value * sign
        top = value.astype(jnp.bfloat16)
        value = value - top.astype(jnp.float32)
        middle = value.astype(jnp.bfloat16)
        low = (value - middle.astype(jnp.float32)).astype(jnp.bfloat16)
        rotated = (dot(low, table) + dot(middle, table)) + dot(top, table)
        rotated = rotated * jnp.float32(1.0 / math.sqrt(HD))
        rotated = rotated.astype(jnp.bfloat16).astype(jnp.float32)
        peak = jnp.max(jnp.abs(rotated), axis=0, keepdims=True)
        power = jnp.floor(jnp.log2(jnp.maximum(peak, 1e-30)))
        rotated = rotated * jnp.exp2(TOP - power)
        out[pl.ds(pl.multiple_of(side * rows, rows), rows), columns] = rotated[:rows]
        out[pl.ds(pl.multiple_of((1 - side) * rows, rows), rows), columns] = rotated[rows:]
        out[2 * rows :, columns] = jnp.broadcast_to(power, (SCALE_ROWS, HD))


def rotate(place, signs, own, other):
    return pl.pallas_call(
        rotate_kernel,
        out_shape=jax.ShapeDtypeStruct((own.shape[0] + SCALE_ROWS, KV), jnp.float32),
        in_specs=[SMEM_SPEC] + [VMEM_SPEC] * 3,
        out_specs=VMEM_SPEC,
        compiler_params=LIMITS,
        name="rotate",
    )(place, signs, own, other)


def stack_heads(query):
    group = query.shape[1] // HD
    return jnp.concatenate([query[:, g * HD : (g + 1) * HD] for g in range(group)], axis=0)


def absorb(state, q, cache, pos, index, first, rows):
    highest, total = state
    group = q.shape[0] // rows
    size = pos.shape[1]
    for step in range(cache.shape[0] // size):
        keys = cache[step * size : (step + 1) * size, :HD]
        value = cache[step * size : (step + 1) * size, HD:]
        scores = lax.dot_general(
            q, keys, (((1,), (1,)), ((), ())), preferred_element_type=jnp.float32
        )
        query_pos = first + lax.broadcasted_iota(jnp.int32, (rows, size), 0)
        allowed = pos[pl.ds(2 * index + step, 1), :] <= query_pos
        scores = jnp.where(allowed[None], scores.reshape(group, rows, size), -jnp.inf)
        scores = scores.reshape(group * rows, size)
        new_high = jnp.maximum(highest, jnp.max(scores, axis=1, keepdims=True))
        weights = jnp.exp2((scores - new_high) * SCORE_SCALE).astype(jnp.bfloat16)
        shrink = jnp.exp2((highest - new_high) * SCORE_SCALE)
        value = jnp.concatenate([value, jnp.ones_like(value)], axis=1)
        total = total * shrink + dot(weights, value)
        highest = new_high
    return highest, total


def fresh(q):
    return (
        jnp.full((q.shape[0], 1), -1e30, jnp.float32),
        jnp.zeros((q.shape[0], KV), jnp.float32),
    )


def finish(state):
    total = state[1]
    return (total[:, :HD] / total[:, HD:]).astype(jnp.bfloat16)


def own_keys_kernel(place, query, pos, own, high_out, total_out):
    q = stack_heads(query)
    core = place[0] & 1
    highest, total = absorb(fresh(q), q, own, pos, core, place[1], query.shape[0])
    high_out[...] = jnp.broadcast_to(highest, high_out.shape)
    total_out[...] = total


def own_keys(place, query, pos, own):
    stacked = query.shape[0] * query.shape[1] // HD
    return pl.pallas_call(
        own_keys_kernel,
        out_shape=(
            jax.ShapeDtypeStruct((stacked, HD), jnp.float32),
            jax.ShapeDtypeStruct((stacked, KV), jnp.float32),
        ),
        in_specs=[SMEM_SPEC] + [VMEM_SPEC] * 3,
        out_specs=(VMEM_SPEC, VMEM_SPEC),
        compiler_params=LIMITS,
        name="own_keys",
    )(place, query, pos, own)


def first_layer_kernel(place, query, pos, mate, high_in, total_in, weight, out):
    q = stack_heads(query)
    rows = query.shape[0]
    core = place[0] & 1
    state = (high_in[:, :1], total_in[...])
    attended = finish(absorb(state, q, mate, pos, 1 - core, place[1], rows))
    first = jnp.concatenate(
        [attended[g : g + rows] for g in range(0, attended.shape[0], rows)], axis=1
    )
    sections, share = weight.shape[0], out.shape[2]
    each = out.shape[0] // sections
    for h in range(out.shape[0]):
        columns = slice((h % each) * share, (h % each + 1) * share)
        out[h] = dot(first, weight[h // each, :, columns]).astype(jnp.bfloat16)


def first_layer(place, query, pos, mate, state, weight, heads):
    rows = query.shape[0]
    share = weight.shape[0] * weight.shape[2] // heads
    return pl.pallas_call(
        first_layer_kernel,
        out_shape=jax.ShapeDtypeStruct((heads, rows, share), jnp.bfloat16),
        in_specs=[SMEM_SPEC] + [VMEM_SPEC] * 6,
        out_specs=VMEM_SPEC,
        compiler_params=LIMITS,
        name="first_layer",
    )(place, query, pos, mate, *state, weight)


def residual_kernel(pieces, hidden, gain, stream, spread):
    total = hidden[...].astype(jnp.float32)
    for h in range(pieces.shape[0]):
        total = total + pieces[h].astype(jnp.float32)
    stream[...] = total.astype(jnp.bfloat16)
    scaled = (total * gain[...]).astype(jnp.bfloat16)
    for h in range(pieces.shape[0]):
        spread[h] = scaled


def residual_sum(pieces, hidden, gain):
    return pl.pallas_call(
        residual_kernel,
        out_shape=(
            jax.ShapeDtypeStruct(hidden.shape, jnp.bfloat16),
            jax.ShapeDtypeStruct(pieces.shape, jnp.bfloat16),
        ),
        in_specs=[VMEM_SPEC] * 3,
        out_specs=(VMEM_SPEC, VMEM_SPEC),
        compiler_params=LIMITS,
        name="residual_sum",
    )(pieces, hidden, gain)


def second_layer_kernel(place, scaled, inverse, weight, pos, own, mate, out):
    heads, rows, share = scaled.shape
    total = jnp.zeros((rows, weight.shape[1]), jnp.float32)
    square = jnp.zeros((rows, 1), jnp.float32)
    for h in range(heads):
        block = scaled[h]
        total = total + dot(block, weight[h * share : (h + 1) * share])
        plain = block.astype(jnp.float32) * inverse[h : h + 1]
        square = square + jnp.sum(plain * plain, axis=1, keepdims=True)
    root = lax.rsqrt(square / (heads * share) + 1e-6)
    q = stack_heads((total * root).astype(jnp.bfloat16))
    core = place[0] & 1
    state = absorb(fresh(q), q, own, pos, core, place[1], rows)
    attended = finish(absorb(state, q, mate, pos, 1 - core, place[1], rows))
    for g in range(out.shape[1] // HD):
        out[:, g * HD : (g + 1) * HD] = attended[g * rows : (g + 1) * rows]


def second_layer(place, scaled, inverse, weight, pos, own, mate):
    return pl.pallas_call(
        second_layer_kernel,
        out_shape=jax.ShapeDtypeStruct((scaled.shape[1], weight.shape[1]), jnp.bfloat16),
        in_specs=[SMEM_SPEC] + [VMEM_SPEC] * 6,
        out_specs=VMEM_SPEC,
        compiler_params=LIMITS,
        name="second_layer",
    )(place, scaled, inverse, weight, pos, own, mate)


def per_device(
    self_hidden, kv_weight, signs, positions, queries, out_weight, query_weight, norm_gain
):
    rows, width = self_hidden.shape
    sections, ctxs, heads = (lax.axis_size(a) for a in ("section", "ctx", "head"))
    section, ctx, head = (lax.axis_index(a) for a in ("section", "ctx", "head"))
    share = width // heads
    depth = width // sections

    def swap_core(value):
        return lax.ppermute(value, "section", [(i, i ^ 1) for i in range(sections)])

    def swap_y(value):
        return lax.ppermute(value, "section", [(i, i ^ 2) for i in range(sections)])

    def swap_far_y(value):
        pairs = [
            (s * heads + h, (s ^ 2) * heads + (h ^ 1))
            for s in range(sections)
            for h in range(heads)
        ]
        return lax.ppermute(value, ("section", "head"), pairs)

    def columns(of):
        return lax.dynamic_slice_in_dim(self_hidden, of * depth, depth, 1)

    first_pos = lax.dynamic_index_in_dim(positions, (section * ctxs + ctx) * rows, 0, False)
    place = jnp.stack([section, first_pos])
    pos = positions.reshape(2, sections // 2, ctxs, rows)
    pos = jnp.transpose(pos, (1, 2, 0, 3)).reshape(sections, ctxs * rows)

    from_near = swap_y(columns(section ^ 2))
    from_far = swap_far_y(columns(section ^ 3))
    mate_weight = swap_core(kv_weight)

    out_all = lax.all_gather(out_weight, "section", axis=0)
    query_all = lax.all_gather(query_weight, "section", axis=0, tiled=True)

    own, send = kv_partial(place, self_hidden, from_near, from_far, kv_weight, mate_weight)
    coded = rotate(place, signs, own, swap_y(send)).astype(jnp.float16)
    coded = lax.all_gather(coded, "ctx", axis=0).astype(jnp.float32)
    power = coded[:, 2 * rows : 2 * rows + 1]
    cache_own = (coded[:, : 2 * rows] * jnp.exp2(power - TOP)).astype(jnp.bfloat16)
    cache_own = cache_own.reshape(ctxs * 2 * rows, KV)
    cache_mate = swap_core(cache_own)

    state = own_keys(place, queries, pos, cache_own)
    partial = first_layer(place, queries, pos, cache_mate, state, out_all, heads)
    pieces = lax.all_to_all(partial, "head", 0, 0, tiled=True)
    own_hidden = lax.dynamic_slice_in_dim(self_hidden, head * share, share, 1)
    gain = norm_gain.astype(jnp.float32)
    own_gain = lax.dynamic_slice_in_dim(gain, head * share, share, 0)
    stream, spread = residual_sum(pieces, own_hidden, own_gain.reshape(1, share))
    scaled_all = lax.all_to_all(spread, "head", 0, 0, tiled=True)
    inverse = (1.0 / gain).reshape(heads, share)
    second = second_layer(place, scaled_all, inverse, query_all, pos, cache_own, cache_mate)
    return (stream, second)


def solution(mesh):
    return jax.shard_map(
        per_device,
        mesh=mesh,
        in_specs=(
            P(("section", "ctx"), None),
            P("section", "head"),
            P("head", None),
            P(),
            P(("section", "ctx"), "head"),
            P("head", "section"),
            P("section", "head"),
            P(),
        ),
        out_specs=(P(("section", "ctx"), "head"), P(("section", "ctx"), "head")),
        check_vma=False,
    )
```

time: 220 us -> 173 us (0.79)
  the two profiles are of different devices: /device:TPU:32 before, /device:TPU:1 now
where the time goes in v2:
time: 173 us; the launch traced here: 172 us
  waiting for transfers between devices  49.1 us (28%)
  blocking collectives  39.5 us (23%)
  starting transfers between devices  34.2 us (20%)
  Pallas kernels  25.5 us (15%)
  between operations  14.3 us (8%)
  local copies, waits for them, and re-layouts  7.87 us (5%)
    all_gather x1, blocking collectives, per_device(): coded = lax.all_gather(coded, 'ctx', axis=0).astype(jnp.float32)  39.5 us
    ppermute x2, starting transfers between devices, swap_core(): return lax.ppermute(value, 'section', [(i, i ^ 1) for i in range(sections)])  19.7 us
    all_to_all x1, waiting for transfers between devices, per_device(): pieces = lax.all_to_all(partial, 'head', 0, 0, tiled=True)  17.2 us
    all_to_all x1, waiting for transfers between devices, per_device(): scaled_all = lax.all_to_all(spread, 'head', 0, 0, tiled=True)  12.9 us
    ppermute x2, waiting for transfers between devices, swap_y(): return lax.ppermute(value, 'section', [(i, i ^ 2) for i in range(sections)])  11.9 us
    pallas_call x1, Pallas kernels, second_layer(): pl.pallas_call(second_layer_kernel, out_shape=jax.ShapeDtypeStruct((scale...  10.8 us
    pallas_call x1, Pallas kernels, first_layer(): pl.pallas_call(first_layer_kernel, out_shape=jax.ShapeDtypeStruct((heads,...  7.63 us
    unnamed x17, local copies, waits for them, and re-layouts  4.46 us
  transfers between devices with their start and end apart: 9, of which 6 were waited for; matrix products, arithmetic and copies ran while one was open for 3% of the time, Pallas kernels for 9%

profile of v2, /device:TPU:1, one launch (start us, length us, event | category | flops | bytes accessed | tf_op | source)
XLA Modules:
  0.0 172.0 jit_solution(10006051565315312941)
XLA Ops:
  7.2 0.7 all-gather.8.cloned.1.call-update
  8.0 0.7 all-gather.6.cloned.1.call-update
  8.7 8.8 %collective-permute-start.2 = (bf16[1024,256]{1,0:T(8,128)(2,1)}, bf16[1024,256]{1,0:T(8,128)(2,1)S(1)}, u32[]{:S(2)}, u32[]{:S(2)}) collective-permute-start(bf16[1024,256]{1,0:T(8,128)(2,1)} %weight.1), channel_id=1, source_target_pairs={{0,128},{128,0},{256,384},{384,256},{1,129},{129,1},{257,385},{385... | collective-permute-start | bytes 1572872 | tf_op jit(solution)/shard_map/ppermute | solution.py:249
  17.5 1.1 constant_dynamic-slice_fusion.1
  18.5 1.9 %collective-permute-start = (bf16[128,1024]{1,0:T(8,128)(2,1)S(1)}, bf16[128,1024]{1,0:T(8,128)(2,1)S(1)}, u32[]{:S(2)}, u32[]{:S(2)}) collective-permute-start(bf16[128,1024]{1,0:T(8,128)(2,1)S(1)} %get-tuple-element.15), channel_id=1, source_target_pairs={{0,256},{128,384},{256,0},{384,128},{1,257},{129,385},{257,1},{385... | collective-permute-start | bytes 786440 | tf_op jit(solution)/shard_map/ppermute | solution.py:252
  20.5 1.9 %collective-permute-start.1 = (bf16[128,1024]{1,0:T(8,128)(2,1)S(1)}, bf16[128,1024]{1,0:T(8,128)(2,1)S(1)}, u32[]{:S(2)}, u32[]{:S(2)}) collective-permute-start(bf16[128,1024]{1,0:T(8,128)(2,1)S(1)} %get-tuple-element.14), channel_id=1, source_target_pairs={{0,257},{1,256},{2,259},{3,258},{4,261},{5,260},{6,263},{7,262},{1... | collective-permute-start | bytes 786440 | tf_op jit(solution)/shard_map/ppermute | solution.py:260
  22.4 1.3 dynamic_slice.16
  23.7 0.7 pad_add_fusion.place
  24.4 4.0 %collective-permute-done.from_near = bf16[128,1024]{1,0:T(8,128)(2,1)S(1)} collective-permute-done((bf16[128,1024]{1,0:T(8,128)(2,1)S(1)}, bf16[128,1024]{1,0:T(8,128)(2,1)S(1)}, u32[]{:S(2)}, u32[]{:S(2)}) %collective-permute-start) | collective-permute-done | bytes 262176 | tf_op jit(solution)/shard_map/ppermute | solution.py:252
  28.4 3.1 %collective-permute-done.1.from_far = bf16[128,1024]{1,0:T(8,128)(2,1)S(1)} collective-permute-done((bf16[128,1024]{1,0:T(8,128)(2,1)S(1)}, bf16[128,1024]{1,0:T(8,128)(2,1)S(1)}, u32[]{:S(2)}, u32[]{:S(2)}) %collective-permute-start.1) | collective-permute-done | bytes 262176 | tf_op jit(solution)/shard_map/ppermute | solution.py:260
  31.5 1.3 copy-done.1
  32.8 1.1 copy-done.4
  33.9 1.0 kv_partial.1
  34.9 1.9 %collective-permute-start.3 = (bf16[256,256]{1,0:T(8,128)(2,1)S(1)}, bf16[256,256]{1,0:T(8,128)(2,1)S(1)}, u32[]{:S(2)}, u32[]{:S(2)}) collective-permute-start(bf16[256,256]{1,0:T(8,128)(2,1)S(1)} %get-tuple-element.9), channel_id=1, source_target_pairs={{0,256},{128,384},{256,0},{384,128},{1,257},{129,385},{257,1},{385... | collective-permute-start | bytes 393224 | tf_op jit(solution)/shard_map/ppermute | solution.py:252
  36.9 8.0 %collective-permute-done.3.other = bf16[256,256]{1,0:T(8,128)(2,1)S(1)} collective-permute-done((bf16[256,256]{1,0:T(8,128)(2,1)S(1)}, bf16[256,256]{1,0:T(8,128)(2,1)S(1)}, u32[]{:S(2)}, u32[]{:S(2)}) %collective-permute-start.3) | collective-permute-done | bytes 131104 | tf_op jit(solution)/shard_map/ppermute | solution.py:252
  44.8 0.9 rotate.1
  45.7 39.5 %all-gather.9 = f16[4352,256]{1,0:T(8,128)(2,1)S(1)} all-gather(f16[272,256]{1,0:T(8,128)(2,1)S(1)} %convert_element_type.12), channel_id=2, replica_groups=mesh['section'=4,'ctx'=16,'head'=8] {'ctx'}, dimensions={0}, use_global_device_ids=true | all-gather | bytes 2367488 | tf_op jit(solution)/shard_map/all_gather | solution.py:279
  85.2 0.4 convert
  85.7 0.4 fusion
  86.1 10.9 %collective-permute-start.4 = (bf16[4096,256]{1,0:T(8,128)(2,1)S(1)}, bf16[4096,256]{1,0:T(8,128)(2,1)}, u32[]{:S(2)}, u32[]{:S(2)}) collective-permute-start(bf16[4096,256]{1,0:T(8,128)(2,1)S(1)} %bitcast.12), channel_id=1, source_target_pairs={{0,128},{128,0},{256,384},{384,256},{1,129},{129,1},{257,385},{385... | collective-permute-start | bytes 6291464 | tf_op jit(solution)/shard_map/ppermute | solution.py:249
  97.2 4.4 %own_keys.1 = (f32[512,128]{1,0:T(8,128)S(1)}, f32[512,256]{1,0:T(8,128)S(1)}) custom-call(s32[2]{0:T(128)S(1)} %pad_add_fusion.place, bf16[128,512]{1,0:T(8,128)(2,1)S(1)} %copy-done.3, s32[4,2048]{1,0:T(4,128)S(1)} %reshape.20.pos, bf16[4096,256]{1,0:T(8,128)(2,1)S(1)} %bitcast.13), custom_call_target="tpu_custom_call" | custom-call | tf_op jit(solution)/shard_map/own_keys/pallas_call | solution.py:144
  101.6 7.6 %first_layer.1 = bf16[8,128,512]{2,1,0:T(8,128)(2,1)S(1)} custom-call(s32[2]{0:T(128)S(1)} %pad_add_fusion.place, bf16[128,512]{1,0:T(8,128)(2,1)S(1)} %copy-done.3, s32[4,2048]{1,0:T(4,128)S(1)} %reshape.20.pos, bf16[4096,256]{1,0:T(8,128)(2,1)} %collective-permute-done.4.mate, f32[512,128]{1,0:T(8,128)S(1)} %get-tuple-element.10.high_in, ...), custom_call_target="tpu_custom_call" | custom-call | tf_op jit(solution)/shard_map/first_layer/pallas_call | solution.py:176
  109.3 1.0 copy-done
  110.3 4.4 %all-to-all-start = ((bf16[8,128,512]{2,1,0:T(8,128)(2,1)}), bf16[8,128,512]{2,1,0:T(8,128)(2,1)S(1)}, u32[]{:S(2)}, u32[]{:S(2)}) async-start(bf16[8,128,512]{2,1,0:T(8,128)(2,1)} %copy-done), calls=%async_computation | async-start | bytes 2097152 | tf_op jit(solution)/shard_map/all_to_all | solution.py:287
  114.8 0.9 constant_dynamic-slice_fusion.hidden
  115.7 17.2 %all-to-all-done.pieces = bf16[8,128,512]{2,1,0:T(8,128)(2,1)S(1)} async-done(((bf16[8,128,512]{2,1,0:T(8,128)(2,1)}), bf16[8,128,512]{2,1,0:T(8,128)(2,1)S(1)}, u32[]{:S(2)}, u32[]{:S(2)}) %all-to-all-start) | async-done | bytes 1048608 | tf_op jit(solution)/shard_map/all_to_all | solution.py:287
  132.9 0.8 residual_sum.1
  133.7 1.0 copy-done.2
  134.7 4.2 %all-to-all-start.1 = ((bf16[8,128,512]{2,1,0:T(8,128)(2,1)}), bf16[8,128,512]{2,1,0:T(8,128)(2,1)S(1)}, u32[]{:S(2)}, u32[]{:S(2)}) async-start(bf16[8,128,512]{2,1,0:T(8,128)(2,1)} %copy-done.2), calls=%async_computation.1 | async-start | bytes 2097152 | tf_op jit(solution)/shard_map/all_to_all | solution.py:292
  138.9 2.6 %all-gather.6.cloned.1.call-done.weight = bf16[4096,512]{1,0:T(8,128)(2,1)} async-done(((bf16[1024,512]{1,0:T(8,128)(2,1)}), bf16[4096,512]{1,0:T(8,128)(2,1)}) %all-gather.6.cloned.1.call-update) | async-done | bytes 4194320 | tf_op jit(solution)/shard_map/all_gather | solution.py:275
  141.5 12.9 %all-to-all-done.1.scaled = bf16[8,128,512]{2,1,0:T(8,128)(2,1)S(1)} async-done(((bf16[8,128,512]{2,1,0:T(8,128)(2,1)}), bf16[8,128,512]{2,1,0:T(8,128)(2,1)S(1)}, u32[]{:S(2)}, u32[]{:S(2)}) %all-to-all-start.1) | async-done | bytes 1048608 | tf_op jit(solution)/shard_map/all_to_all | solution.py:292
  154.4 10.8 %second_layer.1 = bf16[128,512]{1,0:T(8,128)(2,1)} custom-call(s32[2]{0:T(128)S(1)} %pad_add_fusion.place, bf16[8,128,512]{2,1,0:T(8,128)(2,1)S(1)} %all-to-all-done.1.scaled, f32[8,512]{1,0:T(8,128)S(1)} %reshape.23.inverse, bf16[4096,512]{1,0:T(8,128)(2,1)} %all-gather.6.cloned.1.call-done.weight, s32[4,2048]{1,0:T(4,128)S(1)} %reshape.20.pos, ...), custom_call_target="tpu_custom_call" | custom-call | tf_op jit(solution)/shard_map/second_layer/pallas_call | solution.py:229
  (25 shorter events, 0.3 us)
Async XLA Ops:
  7.2 37.7 %copy-start.5 = (s32[1,128]{1,0:T(1,128)S(1)}, s32[1,128]{1,0:T(1,128)}, u32[]{:S(2)}) copy-start(s32[1,128]{1,0:T(1,128)} %signs.1) | copy-start | bytes 1540
  7.2 94.4 %all-gather.8.cloned.1.call-start = ((), (), s32[]{:S(2)}) async-start(), calls=%async_computation.3 | async-start | bytes 5242880 | tf_op jit(solution)/shard_map/all_gather | solution.py:274
  7.9 133.6 %all-gather.6.cloned.1.call-start = ((), (), s32[]{:S(2)}) async-start(), calls=%async_computation.2 | async-start | bytes 5242880 | tf_op jit(solution)/shard_map/all_gather | solution.py:275
  8.7 22.9 %collective-permute-start.2 = (bf16[1024,256]{1,0:T(8,128)(2,1)}, bf16[1024,256]{1,0:T(8,128)(2,1)S(1)}, u32[]{:S(2)}, u32[]{:S(2)}) collective-permute-start(bf16[1024,256]{1,0:T(8,128)(2,1)} %weight.1), channel_id=1, source_target_pairs={{0,128},{128,0},{256,384},{384,256},{1,129},{129,1},{257,385},{385... | collective-permute-start | bytes 1572872 | tf_op jit(solution)/shard_map/ppermute | solution.py:249
  18.5 9.8 %collective-permute-start = (bf16[128,1024]{1,0:T(8,128)(2,1)S(1)}, bf16[128,1024]{1,0:T(8,128)(2,1)S(1)}, u32[]{:S(2)}, u32[]{:S(2)}) collective-permute-start(bf16[128,1024]{1,0:T(8,128)(2,1)S(1)} %get-tuple-element.15), channel_id=1, source_target_pairs={{0,256},{128,384},{256,0},{384,128},{1,257},{129,385},{257,1},{385... | collective-permute-start | bytes 786440 | tf_op jit(solution)/shard_map/ppermute | solution.py:252
  20.5 11.0 %collective-permute-start.1 = (bf16[128,1024]{1,0:T(8,128)(2,1)S(1)}, bf16[128,1024]{1,0:T(8,128)(2,1)S(1)}, u32[]{:S(2)}, u32[]{:S(2)}) collective-permute-start(bf16[128,1024]{1,0:T(8,128)(2,1)S(1)} %get-tuple-element.14), channel_id=1, source_target_pairs={{0,257},{1,256},{2,259},{3,258},{4,261},{5,260},{6,263},{7,262},{1... | collective-permute-start | bytes 786440 | tf_op jit(solution)/shard_map/ppermute | solution.py:260
  31.5 1.3 copy-start.1
  32.8 1.1 copy-start.4
  34.9 9.9 %collective-permute-start.3 = (bf16[256,256]{1,0:T(8,128)(2,1)S(1)}, bf16[256,256]{1,0:T(8,128)(2,1)S(1)}, u32[]{:S(2)}, u32[]{:S(2)}) collective-permute-start(bf16[256,256]{1,0:T(8,128)(2,1)S(1)} %get-tuple-element.9), channel_id=1, source_target_pairs={{0,256},{128,384},{256,0},{384,128},{1,257},{129,385},{257,1},{385... | collective-permute-start | bytes 393224 | tf_op jit(solution)/shard_map/ppermute | solution.py:252
  85.6 11.4 %copy-start.6 = (s32[8192]{0:T(1024)S(1)}, s32[8192]{0:T(1024)}, u32[]{:S(2)}) copy-start(s32[8192]{0:T(1024)} %param.11) | copy-start | bytes 98308
  85.6 11.5 %copy-start.3 = (bf16[128,512]{1,0:T(8,128)(2,1)S(1)}, bf16[128,512]{1,0:T(8,128)(2,1)}, u32[]{:S(2)}) copy-start(bf16[128,512]{1,0:T(8,128)(2,1)} %query.3) | copy-start | bytes 393220
  86.1 15.5 %collective-permute-start.4 = (bf16[4096,256]{1,0:T(8,128)(2,1)S(1)}, bf16[4096,256]{1,0:T(8,128)(2,1)}, u32[]{:S(2)}, u32[]{:S(2)}) collective-permute-start(bf16[4096,256]{1,0:T(8,128)(2,1)S(1)} %bitcast.12), channel_id=1, source_target_pairs={{0,128},{128,0},{256,384},{384,256},{1,129},{129,1},{257,385},{385... | collective-permute-start | bytes 6291464 | tf_op jit(solution)/shard_map/ppermute | solution.py:249
  101.6 13.1 %copy-start.7 = (bf16[4096]{0:T(1024)(128)(2,1)S(1)}, bf16[4096]{0:T(1024)(128)(2,1)}, u32[]{:S(2)}) copy-start(bf16[4096]{0:T(1024)(128)(2,1)} %param.15) | copy-start | bytes 24580
  109.3 1.0 copy-start
  110.3 22.6 %all-to-all-start = ((bf16[8,128,512]{2,1,0:T(8,128)(2,1)}), bf16[8,128,512]{2,1,0:T(8,128)(2,1)S(1)}, u32[]{:S(2)}, u32[]{:S(2)}) async-start(bf16[8,128,512]{2,1,0:T(8,128)(2,1)} %copy-done), calls=%async_computation | async-start | bytes 2097152 | tf_op jit(solution)/shard_map/all_to_all | solution.py:287
  133.7 1.0 copy-start.2
  134.7 19.7 %all-to-all-start.1 = ((bf16[8,128,512]{2,1,0:T(8,128)(2,1)}), bf16[8,128,512]{2,1,0:T(8,128)(2,1)S(1)}, u32[]{:S(2)}, u32[]{:S(2)}) async-start(bf16[8,128,512]{2,1,0:T(8,128)(2,1)} %copy-done.2), calls=%async_computation.1 | async-start | bytes 2097152 | tf_op jit(solution)/shard_map/all_to_all | solution.py:292
Sparse Core Ops, SparseCore 0:
  10.1 62.9 all-gather.7
  75.2 66.2 all-gather.5

commit v3 on v2

--- a/solution.py
+++ b/solution.py
@@ -12,41 +12,66 @@
 SCALE_ROWS = 16
 TOP = 13.0
 SCORE_SCALE = math.log2(math.e) / math.sqrt(HD)
-LIMITS = pltpu.CompilerParams(vmem_limit_bytes=48 * 2**20)
+
+
+def limit(mebibytes):
+    return pltpu.CompilerParams(vmem_limit_bytes=mebibytes * 2**20)
+
 
 SMEM_SPEC = pl.BlockSpec(memory_space=pltpu.SMEM)
 VMEM_SPEC = pl.BlockSpec(memory_space=pltpu.VMEM)
+HBM_SPEC = pl.BlockSpec(memory_space=pltpu.HBM)
+
+
+def in_hbm(value):
+    return pltpu.with_memory_space_constraint(value, pltpu.HBM)
 
 
 def dot(a, b):
     return jnp.dot(a, b, preferred_element_type=jnp.float32)
 
 
-def kv_partial_kernel(place, hidden, from_near, from_far, weight, mate_weight, out, send):
+def kv_own_kernel(place, hidden, weight, mate_weight, out):
     depth = weight.shape[0]
     section = place[0]
     mine = hidden[:, pl.ds(pl.multiple_of(section * depth, depth), depth)]
     mates = hidden[:, pl.ds(pl.multiple_of((section ^ 1) * depth, depth), depth)]
-    both = dot(jnp.concatenate([mine, from_near[...]], axis=0), weight[...]) + dot(
-        jnp.concatenate([mates, from_far[...]], axis=0), mate_weight[...]
-    )
-    out[...] = both
-    send[...] = both.astype(jnp.bfloat16)
-
-
-def kv_partial(place, hidden, from_near, from_far, weight, mate_weight):
-    shape = (2 * hidden.shape[0], weight.shape[1])
-    return pl.pallas_call(
-        kv_partial_kernel,
+    out[...] = dot(mine, weight[...]) + dot(mates, mate_weight[...])
+
+
+def kv_own(place, hidden, weight, mate_weight):
+    return pl.pallas_call(
+        kv_own_kernel,
+        out_shape=jax.ShapeDtypeStruct((hidden.shape[0], weight.shape[1]), jnp.float32),
+        in_specs=[SMEM_SPEC] + [VMEM_SPEC] * 3,
+        out_specs=VMEM_SPEC,
+        compiler_params=limit(16),
+        name="kv_own",
+    )(place, hidden, weight, mate_weight)
+
+
+def kv_near_kernel(own, from_near, from_far, weight, mate_weight, out, send):
+    rows = own.shape[0]
+    near = dot(from_near[...], weight[...]) + dot(from_far[...], mate_weight[...])
+    out[:rows] = own[...]
+    out[rows:] = near
+    send[:rows] = own[...].astype(jnp.bfloat16)
+    send[rows:] = near.astype(jnp.bfloat16)
+
+
+def kv_near(own, from_near, from_far, weight, mate_weight):
+    shape = (2 * own.shape[0], own.shape[1])
+    return pl.pallas_call(
+        kv_near_kernel,
         out_shape=(
             jax.ShapeDtypeStruct(shape, jnp.float32),
             jax.ShapeDtypeStruct(shape, jnp.bfloat16),
         ),
-        in_specs=[SMEM_SPEC] + [VMEM_SPEC] * 5,
+        in_specs=[VMEM_SPEC] * 5,
         out_specs=(VMEM_SPEC, VMEM_SPEC),
-        compiler_params=LIMITS,
-        name="kv_partial",
-    )(place, hidden, from_near, from_far, weight, mate_weight)
+        compiler_params=limit(16),
+        name="kv_near",
+    )(own, from_near, from_far, weight, mate_weight)
 
 
 def rotate_kernel(place, signs, own, other, out):
@@ -86,7 +111,7 @@
         out_shape=jax.ShapeDtypeStruct((own.shape[0] + SCALE_ROWS, KV), jnp.float32),
         in_specs=[SMEM_SPEC] + [VMEM_SPEC] * 3,
         out_specs=VMEM_SPEC,
-        compiler_params=LIMITS,
+        compiler_params=limit(16),
         name="rotate",
     )(place, signs, own, other)
 
@@ -96,11 +121,13 @@
     return jnp.concatenate([query[:, g * HD : (g + 1) * HD] for g in range(group)], axis=0)
 
 
-def absorb(state, q, cache, pos, index, first, rows):
+def absorb(state, q, cache, pos, index, first, rows, loads=()):
     highest, total = state
     group = q.shape[0] // rows
     size = pos.shape[1]
     for step in range(cache.shape[0] // size):
+        if loads:
+            loads[step].wait()
         keys = cache[step * size : (step + 1) * size, :HD]
         value = cache[step * size : (step + 1) * size, HD:]
         scores = lax.dot_general(
@@ -119,6 +146,16 @@
     return highest, total
 
 
+def load_rows(source, target, sem, parts):
+    size = source.shape[0] // parts
+    copies = []
+    for i in range(parts):
+        rows = pl.ds(i * size, size)
+        copies.append(pltpu.make_async_copy(source.at[rows], target.at[rows], sem.at[i]))
+        copies[-1].start()
+    return copies
+
+
 def fresh(q):
     return (
         jnp.full((q.shape[0], 1), -1e30, jnp.float32),
@@ -144,53 +181,80 @@
     return pl.pallas_call(
         own_keys_kernel,
         out_shape=(
-            jax.ShapeDtypeStruct((stacked, HD), jnp.float32),
-            jax.ShapeDtypeStruct((stacked, KV), jnp.float32),
+            pltpu.VMEM((stacked, HD), jnp.float32),
+            pltpu.VMEM((stacked, KV), jnp.float32),
         ),
         in_specs=[SMEM_SPEC] + [VMEM_SPEC] * 3,
         out_specs=(VMEM_SPEC, VMEM_SPEC),
-        compiler_params=LIMITS,
+        compiler_params=limit(24),
         name="own_keys",
     )(place, query, pos, own)
 
 
-def first_layer_kernel(place, query, pos, mate, high_in, total_in, weight, out):
+def first_layer_kernel(
+    place, query, pos, high_in, total_in, mate, weight, out, near, held, stage, mate_sem, sem, out_sem
+):
+    sections = weight.shape[0]
+    mate_loads = load_rows(mate, near, mate_sem, mate.shape[0] // pos.shape[1])
+    loads = load_rows(weight, held, sem, sections)
     q = stack_heads(query)
     rows = query.shape[0]
     core = place[0] & 1
     state = (high_in[:, :1], total_in[...])
-    attended = finish(absorb(state, q, mate, pos, 1 - core, place[1], rows))
+    state = absorb(state, q, near, pos, 1 - core, place[1], rows, mate_loads)
+    attended = finish(state)
     first = jnp.concatenate(
         [attended[g : g + rows] for g in range(0, attended.shape[0], rows)], axis=1
     )
-    sections, share = weight.shape[0], out.shape[2]
-    each = out.shape[0] // sections
-    for h in range(out.shape[0]):
+    heads, _, share = stage.shape
+    each = heads // sections
+    stores = []
+    for h in range(heads):
+        if h % each == 0:
+            loads[h // each].wait()
         columns = slice((h % each) * share, (h % each + 1) * share)
-        out[h] = dot(first, weight[h // each, :, columns]).astype(jnp.bfloat16)
-
-
-def first_layer(place, query, pos, mate, state, weight, heads):
+        stage[h] = dot(first, held[h // each, :, columns]).astype(jnp.bfloat16)
+        stores.append(pltpu.make_async_copy(stage.at[h], out.at[h], out_sem.at[h]))
+        stores[-1].start()
+    for store in stores:
+        store.wait()
+
+
+def first_layer(place, query, pos, state, mate, weight, heads):
     rows = query.shape[0]
-    share = weight.shape[0] * weight.shape[2] // heads
+    sections, _, width = weight.shape
+    shape = (heads, rows, sections * width // heads)
     return pl.pallas_call(
         first_layer_kernel,
-        out_shape=jax.ShapeDtypeStruct((heads, rows, share), jnp.bfloat16),
-        in_specs=[SMEM_SPEC] + [VMEM_SPEC] * 6,
-        out_specs=VMEM_SPEC,
-        compiler_params=LIMITS,
+        out_shape=pltpu.HBM(shape, jnp.bfloat16),
+        in_specs=[SMEM_SPEC] + [VMEM_SPEC] * 4 + [HBM_SPEC] * 2,
+        out_specs=HBM_SPEC,
+        scratch_shapes=[
+            pltpu.VMEM(mate.shape, jnp.bfloat16),
+            pltpu.VMEM(weight.shape, jnp.bfloat16),
+            pltpu.VMEM(shape, jnp.bfloat16),
+            pltpu.SemaphoreType.DMA((mate.shape[0] // pos.shape[1],)),
+            pltpu.SemaphoreType.DMA((sections,)),
+            pltpu.SemaphoreType.DMA((heads,)),
+        ],
+        compiler_params=limit(32),
         name="first_layer",
-    )(place, query, pos, mate, *state, weight)
-
-
-def residual_kernel(pieces, hidden, gain, stream, spread):
+    )(place, query, pos, *state, in_hbm(mate), in_hbm(weight))
+
+
+def residual_kernel(pieces, hidden, gain, stream, spread, scaled, sem):
     total = hidden[...].astype(jnp.float32)
     for h in range(pieces.shape[0]):
         total = total + pieces[h].astype(jnp.float32)
+    scaled[...] = (total * gain[...]).astype(jnp.bfloat16)
+    stores = [
+        pltpu.make_async_copy(scaled, spread.at[h], sem.at[h]) for h in range(spread.shape[0])
+    ]
+    for store in stores:
+        store.start()
     stream[...] = total.astype(jnp.bfloat16)
-    scaled = (total * gain[...]).astype(jnp.bfloat16)
-    for h in range(pieces.shape[0]):
-        spread[h] = scaled
+    for store in stores:
+        store.wait()
 
 
 def residual_sum(pieces, hidden, gain):
@@ -198,42 +262,67 @@
         residual_kernel,
         out_shape=(
             jax.ShapeDtypeStruct(hidden.shape, jnp.bfloat16),
-            jax.ShapeDtypeStruct(pieces.shape, jnp.bfloat16),
+            pltpu.HBM(pieces.shape, jnp.bfloat16),
         ),
         in_specs=[VMEM_SPEC] * 3,
-        out_specs=(VMEM_SPEC, VMEM_SPEC),
-        compiler_params=LIMITS,
+        out_specs=(VMEM_SPEC, HBM_SPEC),
+        scratch_shapes=[
+            pltpu.VMEM(hidden.shape, jnp.bfloat16),
+            pltpu.SemaphoreType.DMA((pieces.shape[0],)),
+        ],
+        compiler_params=limit(16),
         name="residual_sum",
     )(pieces, hidden, gain)
 
 
-def second_layer_kernel(place, scaled, inverse, weight, pos, own, mate, out):
+def second_layer_kernel(
+    place, scaled, inverse, pos, own, near, far, mate, out, held, other, sem, mate_sem
+):
     heads, rows, share = scaled.shape
-    total = jnp.zeros((rows, weight.shape[1]), jnp.float32)
+    half = heads // 2
+    each = half // near.shape[0]
+    core, side = place[0] & 1, place[0] >> 1
+    loads = [
+        load_rows(weight, held.at[i], sem.at[i], weight.shape[0])
+        for i, weight in enumerate((near, far))
+    ]
+    mate_loads = load_rows(mate, other, mate_sem, mate.shape[0] // pos.shape[1])
     square = jnp.zeros((rows, 1), jnp.float32)
     for h in range(heads):
-        block = scaled[h]
-        total = total + dot(block, weight[h * share : (h + 1) * share])
-        plain = block.astype(jnp.float32) * inverse[h : h + 1]
+        plain = scaled[h].astype(jnp.float32) * inverse[h : h + 1]
         square = square + jnp.sum(plain * plain, axis=1, keepdims=True)
     root = lax.rsqrt(square / (heads * share) + 1e-6)
+    total = jnp.zeros((rows, near.shape[2]), jnp.float32)
+    for i in range(2):
+        for k in range(half):
+            if k % each == 0:
+                loads[i][k // each].wait()
+            part = held[i, k // each, (k % each) * share : (k % each + 1) * share]
+            total = total + dot(scaled[(side ^ i) * half + k], part)
     q = stack_heads((total * root).astype(jnp.bfloat16))
-    core = place[0] & 1
     state = absorb(fresh(q), q, own, pos, core, place[1], rows)
-    attended = finish(absorb(state, q, mate, pos, 1 - core, place[1], rows))
+    state = absorb(state, q, other, pos, 1 - core, place[1], rows, mate_loads)
+    attended = finish(state)
     for g in range(out.shape[1] // HD):
         out[:, g * HD : (g + 1) * HD] = attended[g * rows : (g + 1) * rows]
 
 
-def second_layer(place, scaled, inverse, weight, pos, own, mate):
+def second_layer(place, scaled, inverse, pos, own, near, far, mate):
+    parts = mate.shape[0] // pos.shape[1]
     return pl.pallas_call(
         second_layer_kernel,
-        out_shape=jax.ShapeDtypeStruct((scaled.shape[1], weight.shape[1]), jnp.bfloat16),
-        in_specs=[SMEM_SPEC] + [VMEM_SPEC] * 6,
+        out_shape=jax.ShapeDtypeStruct((scaled.shape[1], near.shape[2]), jnp.bfloat16),
+        in_specs=[SMEM_SPEC] + [VMEM_SPEC] * 4 + [HBM_SPEC] * 3,
         out_specs=VMEM_SPEC,
-        compiler_params=LIMITS,
+        scratch_shapes=[
+            pltpu.VMEM((2,) + near.shape, jnp.bfloat16),
+            pltpu.VMEM(mate.shape, jnp.bfloat16),
+            pltpu.SemaphoreType.DMA((2, near.shape[0])),
+            pltpu.SemaphoreType.DMA((parts,)),
+        ],
+        compiler_params=limit(36),
         name="second_layer",
-    )(place, scaled, inverse, weight, pos, own, mate)
+    )(place, scaled, inverse, pos, own, in_hbm(near), in_hbm(far), in_hbm(mate))
 
 
 def per_device(
@@ -262,36 +351,57 @@
     def columns(of):
         return lax.dynamic_slice_in_dim(self_hidden, of * depth, depth, 1)
 
+    here = section.reshape(1)
     first_pos = lax.dynamic_index_in_dim(positions, (section * ctxs + ctx) * rows, 0, False)
     place = jnp.stack([section, first_pos])
     pos = positions.reshape(2, sections // 2, ctxs, rows)
     pos = jnp.transpose(pos, (1, 2, 0, 3)).reshape(sections, ctxs * rows)
 
-    from_near = swap_y(columns(section ^ 2))
-    from_far = swap_far_y(columns(section ^ 3))
-    mate_weight = swap_core(kv_weight)
-
+    def pair(value):
+        groups = [[i, i + 1] for i in range(0, sections, 2)]
+        return lax.all_gather(value, "section", axis=0, axis_index_groups=groups)
+
+    near_columns = columns(section ^ 2)
+    far_columns = columns(section ^ 3)
+    from_near = swap_y(near_columns)
+    from_far = swap_far_y(far_columns)
+    near_columns, far_columns, moved_weight = lax.optimization_barrier(
+        (near_columns, far_columns, kv_weight)
+    )
+    mate_weight = swap_core(moved_weight)
+    own_hidden = lax.dynamic_slice_in_dim(self_hidden, head * share, share, 1)
+    mate_weight, own_hidden = lax.optimization_barrier((mate_weight, own_hidden))
+    own = kv_own(here, self_hidden, kv_weight, mate_weight)
+    own, send = kv_near(own, from_near, from_far, kv_weight, mate_weight)
+    other = swap_y(send)
     out_all = lax.all_gather(out_weight, "section", axis=0)
-    query_all = lax.all_gather(query_weight, "section", axis=0, tiled=True)
-
-    own, send = kv_partial(place, self_hidden, from_near, from_far, kv_weight, mate_weight)
-    coded = rotate(place, signs, own, swap_y(send)).astype(jnp.float16)
-    coded = lax.all_gather(coded, "ctx", axis=0).astype(jnp.float32)
+    query_near = pair(query_weight)
+    send, moved_query = lax.optimization_barrier((send, query_weight))
+    query_far = swap_y(moved_query)
+    gain = norm_gain.astype(jnp.float32)
+    own_gain = lax.dynamic_slice_in_dim(gain, head * share, share, 0).reshape(1, share)
+    inverse = (1.0 / gain).reshape(heads, share)
+    other, place, pos, own_gain, inverse = lax.optimization_barrier(
+        (other, place, pos, own_gain, inverse)
+    )
+    turned = rotate(here, signs, own, other).astype(jnp.float16)
+    coded = lax.all_gather(turned, "ctx", axis=0)
+    coded, query_far = lax.optimization_barrier((coded, query_far))
+    coded = coded.astype(jnp.float32)
     power = coded[:, 2 * rows : 2 * rows + 1]
     cache_own = (coded[:, : 2 * rows] * jnp.exp2(power - TOP)).astype(jnp.bfloat16)
     cache_own = cache_own.reshape(ctxs * 2 * rows, KV)
     cache_mate = swap_core(cache_own)
-
     state = own_keys(place, queries, pos, cache_own)
-    partial = first_layer(place, queries, pos, cache_mate, state, out_all, heads)
+    partial = first_layer(place, queries, pos, state, cache_mate, out_all, heads)
     pieces = lax.all_to_all(partial, "head", 0, 0, tiled=True)
-    own_hidden = lax.dynamic_slice_in_dim(self_hidden, head * share, share, 1)
-    gain = norm_gain.astype(jnp.float32)
-    own_gain = lax.dynamic_slice_in_dim(gain, head * share, share, 0)
-    stream, spread = residual_sum(pieces, own_hidden, own_gain.reshape(1, share))
+    pieces, query_far = lax.optimization_barrier((pieces, query_far))
+    query_far = pair(query_far)
+    stream, spread = residual_sum(pieces, own_hidden, own_gain)
     scaled_all = lax.all_to_all(spread, "head", 0, 0, tiled=True)
-    inverse = (1.0 / gain).reshape(heads, share)
-    second = second_layer(place, scaled_all, inverse, query_all, pos, cache_own, cache_mate)
+    second = second_layer(
+        place, scaled_all, inverse, pos, cache_own, query_near, query_far, cache_mate
+    )
     return (stream, second)
 
 

time: 173 us -> 170 us (0.983)
  waiting for transfers between devices: 49.1 us -> 26.7 us
  blocking collectives: 39.5 us -> 61.7 us
  Pallas kernels: 25.5 us -> 30.5 us
  starting transfers between devices: 34.2 us -> 29.5 us
  local copies, waits for them, and re-layouts: 7.87 us -> 5.01 us
    all_to_all x0 -> x1, blocking collectives: none -> 20.8 us  [per_device(): pieces = lax.all_to_all(partial, 'head', 0, 0, tiled=True)]
    all_to_all x1 -> x0, waiting for transfers between devices: 17.2 us -> none  [per_device(): pieces = lax.all_to_all(partial, 'head', 0, 0, tiled=True)]
    ppermute x2 -> x3, waiting for transfers between devices: 11.9 us -> 7.49 us  [swap_y(): return lax.ppermute(value, 'section', [(i, i ^ 2) for i in range(sections)])]
    all_to_all x1 -> x0, starting transfers between devices: 4.41 us -> none  [per_device(): pieces = lax.all_to_all(partial, 'head', 0, 0, tiled=True)]
    ppermute x2, starting transfers between devices: 19.7 us -> 16.3 us  [swap_core(): return lax.ppermute(value, 'section', [(i, i ^ 1) for i in range(sections)])]
    ppermute x2 -> x3, starting transfers between devices: 3.84 us -> 7.19 us  [swap_y(): return lax.ppermute(value, 'section', [(i, i ^ 2) for i in range(sections)])]
    all_gather x1 -> x2, waiting for transfers between devices: 2.56 us -> 0.02 us  [pair(): return lax.all_gather(value, 'section', axis=0, axis_index_groups=groups)]
    all_to_all x1, waiting for transfers between devices: 12.9 us -> 15.3 us  [per_device(): scaled_all = lax.all_to_all(spread, 'head', 0, 0, tiled=True)]
  transfers between devices with their start and end apart: 9 -> 10, of which waited for: 6 -> 5; matrix products, arithmetic and copies ran while one was open for 3% -> 3% of each run, Pallas kernels for 9% -> 10%
where the time goes in v3:
time: 170 us; the launch traced here: 169 us
  blocking collectives  61.7 us (36%)
  Pallas kernels  30.5 us (18%)
  starting transfers between devices  29.5 us (17%)
  waiting for transfers between devices  26.7 us (16%)
  between operations  14.1 us (8%)
  local copies, waits for them, and re-layouts  5.01 us (3%)
    all_gather x1, blocking collectives, per_device(): coded = lax.all_gather(turned, 'ctx', axis=0)  40.8 us
    all_to_all x1, blocking collectives, per_device(): pieces = lax.all_to_all(partial, 'head', 0, 0, tiled=True)  20.8 us
    ppermute x2, starting transfers between devices, swap_core(): return lax.ppermute(value, 'section', [(i, i ^ 1) for i in range(sections)])  16.3 us
    all_to_all x1, waiting for transfers between devices, per_device(): scaled_all = lax.all_to_all(spread, 'head', 0, 0, tiled=True)  15.3 us
    pallas_call x1, Pallas kernels, second_layer(): pl.pallas_call(second_layer_kernel, out_shape=jax.ShapeDtypeStruct((scale...  13.1 us
    pallas_call x1, Pallas kernels, first_layer(): pl.pallas_call(first_layer_kernel, out_shape=pltpu.HBM(shape, jnp.bfloat1...  10.2 us
    ppermute x3, waiting for transfers between devices, swap_y(): return lax.ppermute(value, 'section', [(i, i ^ 2) for i in range(sections)])  7.49 us
    ppermute x3, starting transfers between devices, swap_y(): return lax.ppermute(value, 'section', [(i, i ^ 2) for i in range(sections)])  7.19 us
  transfers between devices with their start and end apart: 10, of which 5 were waited for; matrix products, arithmetic and copies ran while one was open for 3% of the time, Pallas kernels for 10%

profile of v3, /device:TPU:1, one launch (start us, length us, event | category | flops | bytes accessed | tf_op | source)
XLA Modules:
  0.0 169.1 jit_solution(14070740802218680704)
XLA Ops:
  7.3 0.7 all-gather.9.cloned.1.call-update
  8.0 1.1 constant_dynamic-slice_fusion.1
  9.1 8.8 %collective-permute-start = (bf16[1024,256]{1,0:T(8,128)(2,1)}, bf16[1024,256]{1,0:T(8,128)(2,1)S(1)}, u32[]{:S(2)}, u32[]{:S(2)}) collective-permute-start(bf16[1024,256]{1,0:T(8,128)(2,1)} %weight.3), channel_id=1, source_target_pairs={{0,128},{128,0},{256,384},{384,256},{1,129},{129,1},{257,385},{385... | collective-permute-start | bytes 1572872 | tf_op jit(solution)/shard_map/ppermute | solution.py:338
  17.9 1.9 %collective-permute-start.1 = (bf16[128,1024]{1,0:T(8,128)(2,1)S(1)}, bf16[128,1024]{1,0:T(8,128)(2,1)S(1)}, u32[]{:S(2)}, u32[]{:S(2)}) collective-permute-start(bf16[128,1024]{1,0:T(8,128)(2,1)S(1)} %get-tuple-element.41), channel_id=1, source_target_pairs={{0,256},{128,384},{256,0},{384,128},{1,257},{129,385},{257,1},{385... | collective-permute-start | bytes 786440 | tf_op jit(solution)/shard_map/ppermute | solution.py:341
  19.8 1.9 %collective-permute-start.2 = (bf16[128,1024]{1,0:T(8,128)(2,1)S(1)}, bf16[128,1024]{1,0:T(8,128)(2,1)S(1)}, u32[]{:S(2)}, u32[]{:S(2)}) collective-permute-start(bf16[128,1024]{1,0:T(8,128)(2,1)S(1)} %get-tuple-element.40), channel_id=1, source_target_pairs={{0,257},{1,256},{2,259},{3,258},{4,261},{5,260},{6,263},{7,262},{1... | collective-permute-start | bytes 786440 | tf_op jit(solution)/shard_map/ppermute | solution.py:349
  21.7 0.9 constant_dynamic-slice_fusion.hidden
  22.7 1.2 copy-done
  23.9 1.0 copy-done.1
  24.9 0.3 kv_own.1.own
  25.3 2.4 %collective-permute-done.1.from_near = bf16[128,1024]{1,0:T(8,128)(2,1)S(1)} collective-permute-done((bf16[128,1024]{1,0:T(8,128)(2,1)S(1)}, bf16[128,1024]{1,0:T(8,128)(2,1)S(1)}, u32[]{:S(2)}, u32[]{:S(2)}) %collective-permute-start.1) | collective-permute-done | bytes 262176 | tf_op jit(solution)/shard_map/ppermute | solution.py:341
  27.7 3.1 %collective-permute-done.2.from_far = bf16[128,1024]{1,0:T(8,128)(2,1)S(1)} collective-permute-done((bf16[128,1024]{1,0:T(8,128)(2,1)S(1)}, bf16[128,1024]{1,0:T(8,128)(2,1)S(1)}, u32[]{:S(2)}, u32[]{:S(2)}) %collective-permute-start.2) | collective-permute-done | bytes 262176 | tf_op jit(solution)/shard_map/ppermute | solution.py:349
  30.8 0.3 kv_near.1
  31.2 1.9 %collective-permute-start.3 = (bf16[256,256]{1,0:T(8,128)(2,1)S(1)}, bf16[256,256]{1,0:T(8,128)(2,1)S(1)}, u32[]{:S(2)}, u32[]{:S(2)}) collective-permute-start(bf16[256,256]{1,0:T(8,128)(2,1)S(1)} %get-tuple-element.23), channel_id=1, source_target_pairs={{0,256},{128,384},{256,0},{384,128},{1,257},{129,385},{257,1},{385... | collective-permute-start | bytes 393224 | tf_op jit(solution)/shard_map/ppermute | solution.py:341
  33.1 0.6 dynamic_slice.19
  33.7 3.4 %collective-permute-start.4 = (bf16[1024,512]{1,0:T(8,128)(2,1)S(1)}, bf16[1024,512]{1,0:T(8,128)(2,1)}, u32[]{:S(2)}, u32[]{:S(2)}) collective-permute-start(bf16[1024,512]{1,0:T(8,128)(2,1)S(1)} %copy-done.5), channel_id=1, source_target_pairs={{0,256},{128,384},{256,0},{384,128},{1,257},{129,385},{257,1},{385... | collective-permute-start | bytes 3145736 | tf_op jit(solution)/shard_map/ppermute | solution.py:341
  37.1 0.7 pad_add_fusion.place
  37.8 0.1 dynamic_slice.20
  38.0 1.3 collective-permute-done.3.other
  39.3 0.3 rotate.1
  39.6 40.8 %all-gather.14 = f16[4352,256]{1,0:T(8,128)(2,1)S(1)} all-gather(f16[272,256]{1,0:T(8,128)(2,1)S(1)} %convert_element_type.13), channel_id=2, replica_groups=mesh['section'=4,'ctx'=16,'head'=8] {'ctx'}, dimensions={0}, use_global_device_ids=true | all-gather | bytes 2367488 | tf_op jit(solution)/shard_map/all_gather | solution.py:388
  80.5 3.7 %collective-permute-done.4 = bf16[1024,512]{1,0:T(8,128)(2,1)} collective-permute-done((bf16[1024,512]{1,0:T(8,128)(2,1)S(1)}, bf16[1024,512]{1,0:T(8,128)(2,1)}, u32[]{:S(2)}, u32[]{:S(2)}) %collective-permute-start.4) | collective-permute-done | bytes 1048608 | tf_op jit(solution)/shard_map/ppermute | solution.py:341
  84.2 0.4 convert_element_type.14
  84.7 0.4 fusion
  85.2 7.5 %collective-permute-start.5 = (bf16[4096,256]{1,0:T(8,128)(2,1)S(1)}, bf16[4096,256]{1,0:T(8,128)(2,1)}, u32[]{:S(2)}, u32[]{:S(2)}) collective-permute-start(bf16[4096,256]{1,0:T(8,128)(2,1)S(1)} %bitcast.13), channel_id=1, source_target_pairs={{0,128},{128,0},{256,384},{384,256},{1,129},{129,1},{257,385},{385... | collective-permute-start | bytes 6291464 | tf_op jit(solution)/shard_map/ppermute | solution.py:338
  92.7 0.2 all-gather.13.cloned.1.call-start
  92.9 4.5 %own_keys.1 = (f32[512,128]{1,0:T(8,128)S(1)}, f32[512,256]{1,0:T(8,128)S(1)}) custom-call(s32[2]{0:T(128)S(1)} %pad_add_fusion.place, bf16[128,512]{1,0:T(8,128)(2,1)S(1)} %copy-done.3, s32[4,2048]{1,0:T(4,128)S(1)} %reshape.24.pos, bf16[4096,256]{1,0:T(8,128)(2,1)S(1)} %bitcast.14), custom_call_target="tpu_custom_call" | custom-call | tf_op jit(solution)/shard_map/own_keys/pallas_call | solution.py:181
  97.4 10.2 %first_layer.1 = bf16[8,128,512]{2,1,0:T(8,128)(2,1)} custom-call(s32[2]{0:T(128)S(1)} %pad_add_fusion.place, bf16[128,512]{1,0:T(8,128)(2,1)S(1)} %copy-done.3, s32[4,2048]{1,0:T(4,128)S(1)} %reshape.24.pos, f32[512,128]{1,0:T(8,128)S(1)} %get-tuple-element.30.high_in, f32[512,256]{1,0:T(8,128)S(1)} %get-tuple-element.31.total_in, ...), custom_call_target="tpu_custom_call" | custom-call | tf_op jit(solution)/shard_map/first_layer/pallas_call | solution.py:227
  107.6 20.8 %all_to_all.10.pieces = bf16[8,128,512]{2,1,0:T(8,128)(2,1)S(1)} all-to-all(bf16[8,128,512]{2,1,0:T(8,128)(2,1)} %first_layer.1), channel_id=1, replica_groups=mesh['section'=4,'ctx'=16,'head'=8] {'head'}, dimensions={0} | all-to-all | bytes 2097152 | tf_op jit(solution)/shard_map/all_to_all | solution.py:397
  128.4 1.9 %residual_sum.1 = (bf16[128,512]{1,0:T(8,128)(2,1)}, bf16[8,128,512]{2,1,0:T(8,128)(2,1)}) custom-call(bf16[8,128,512]{2,1,0:T(8,128)(2,1)S(1)} %all_to_all.10.pieces, bf16[128,512]{1,0:T(8,128)(2,1)S(1)} %constant_dynamic-slice_fusion.hidden, f32[1,512]{1,0:T(1,128)S(1)} %bitcast.16), custom_call_target="tpu_custom_call" | custom-call | tf_op jit(solution)/shard_map/residual_sum/pallas_call | solution.py:261
  130.3 3.8 %all-to-all-start.1 = ((bf16[8,128,512]{2,1,0:T(8,128)(2,1)}), bf16[8,128,512]{2,1,0:T(8,128)(2,1)S(1)}, u32[]{:S(2)}, u32[]{:S(2)}) async-start(bf16[8,128,512]{2,1,0:T(8,128)(2,1)} %get-tuple-element.37), calls=%async_computation.1 | async-start | bytes 2097152 | tf_op jit(solution)/shard_map/all_to_all | solution.py:401
  134.2 15.3 %all-to-all-done.1.scaled = bf16[8,128,512]{2,1,0:T(8,128)(2,1)S(1)} async-done(((bf16[8,128,512]{2,1,0:T(8,128)(2,1)}), bf16[8,128,512]{2,1,0:T(8,128)(2,1)S(1)}, u32[]{:S(2)}, u32[]{:S(2)}) %all-to-all-start.1) | async-done | bytes 1048608 | tf_op jit(solution)/shard_map/all_to_all | solution.py:401
  149.5 13.1 %second_layer.1 = bf16[128,512]{1,0:T(8,128)(2,1)} custom-call(s32[2]{0:T(128)S(1)} %pad_add_fusion.place, bf16[8,128,512]{2,1,0:T(8,128)(2,1)S(1)} %all-to-all-done.1.scaled, f32[8,512]{1,0:T(8,128)S(1)} %reshape.26.inverse, s32[4,2048]{1,0:T(4,128)S(1)} %reshape.24.pos, bf16[4096,256]{1,0:T(8,128)(2,1)S(1)} %bitcast.15, bf16[2,1024,512]{2,1,0:T(8,128)(2,1)} %bitcast.19, ...), custom_call_target="tpu_custom_call" | custom-call | tf_op jit(solution)/shard_map/second_layer/pallas_call | solution.py:312
  (30 shorter events, 0.3 us)
Async XLA Ops:
  7.2 23.7 %copy-start.2 = (bf16[1024,256]{1,0:T(8,128)(2,1)S(1)}, bf16[1024,256]{1,0:T(8,128)(2,1)}, u32[]{:S(2)}) copy-start(bf16[1024,256]{1,0:T(8,128)(2,1)} %weight.3) | copy-start | bytes 1572868
  7.2 25.9 %copy-start.7 = (bf16[4096]{0:T(1024)(128)(2,1)S(1)}, bf16[4096]{0:T(1024)(128)(2,1)}, u32[]{:S(2)}) copy-start(bf16[4096]{0:T(1024)(128)(2,1)} %param.15) | copy-start | bytes 24580
  7.2 25.9 %copy-start.6 = (s32[8192]{0:T(1024)S(1)}, s32[8192]{0:T(1024)}, u32[]{:S(2)}) copy-start(s32[8192]{0:T(1024)} %param.11) | copy-start | bytes 98308
  7.2 26.5 %copy-start.5 = (bf16[1024,512]{1,0:T(8,128)(2,1)S(1)}, bf16[1024,512]{1,0:T(8,128)(2,1)}, u32[]{:S(2)}) copy-start(bf16[1024,512]{1,0:T(8,128)(2,1)} %param.14) | copy-start | bytes 3145732
  7.2 32.1 %copy-start.4 = (s32[1,128]{1,0:T(1,128)S(1)}, s32[1,128]{1,0:T(1,128)}, u32[]{:S(2)}) copy-start(s32[1,128]{1,0:T(1,128)} %signs.1) | copy-start | bytes 1540
  7.2 90.2 %all-gather.9.cloned.1.call-start = ((), (), s32[]{:S(2)}) async-start(), calls=%async_computation.2 | async-start | bytes 5242880 | tf_op jit(solution)/shard_map/all_gather | solution.py:377
  8.0 126.2 %all-gather.11.cloned.1.call-start = ((), (), s32[]{:S(2)}) async-start(), calls=%async_computation.3 | async-start | bytes 3145728 | tf_op jit(solution)/shard_map/all_gather | solution.py:362
  9.1 13.6 %collective-permute-start = (bf16[1024,256]{1,0:T(8,128)(2,1)}, bf16[1024,256]{1,0:T(8,128)(2,1)S(1)}, u32[]{:S(2)}, u32[]{:S(2)}) collective-permute-start(bf16[1024,256]{1,0:T(8,128)(2,1)} %weight.3), channel_id=1, source_target_pairs={{0,128},{128,0},{256,384},{384,256},{1,129},{129,1},{257,385},{385... | collective-permute-start | bytes 1572872 | tf_op jit(solution)/shard_map/ppermute | solution.py:338
  17.9 9.8 %collective-permute-start.1 = (bf16[128,1024]{1,0:T(8,128)(2,1)S(1)}, bf16[128,1024]{1,0:T(8,128)(2,1)S(1)}, u32[]{:S(2)}, u32[]{:S(2)}) collective-permute-start(bf16[128,1024]{1,0:T(8,128)(2,1)S(1)} %get-tuple-element.41), channel_id=1, source_target_pairs={{0,256},{128,384},{256,0},{384,128},{1,257},{129,385},{257,1},{385... | collective-permute-start | bytes 786440 | tf_op jit(solution)/shard_map/ppermute | solution.py:341
  19.8 11.0 %collective-permute-start.2 = (bf16[128,1024]{1,0:T(8,128)(2,1)S(1)}, bf16[128,1024]{1,0:T(8,128)(2,1)S(1)}, u32[]{:S(2)}, u32[]{:S(2)}) collective-permute-start(bf16[128,1024]{1,0:T(8,128)(2,1)S(1)} %get-tuple-element.40), channel_id=1, source_target_pairs={{0,257},{1,256},{2,259},{3,258},{4,261},{5,260},{6,263},{7,262},{1... | collective-permute-start | bytes 786440 | tf_op jit(solution)/shard_map/ppermute | solution.py:349
  22.7 1.2 copy-start
  23.9 1.0 copy-start.1
  31.2 8.1 %collective-permute-start.3 = (bf16[256,256]{1,0:T(8,128)(2,1)S(1)}, bf16[256,256]{1,0:T(8,128)(2,1)S(1)}, u32[]{:S(2)}, u32[]{:S(2)}) collective-permute-start(bf16[256,256]{1,0:T(8,128)(2,1)S(1)} %get-tuple-element.23), channel_id=1, source_target_pairs={{0,256},{128,384},{256,0},{384,128},{1,257},{129,385},{257,1},{385... | collective-permute-start | bytes 393224 | tf_op jit(solution)/shard_map/ppermute | solution.py:341
  33.7 50.5 %collective-permute-start.4 = (bf16[1024,512]{1,0:T(8,128)(2,1)S(1)}, bf16[1024,512]{1,0:T(8,128)(2,1)}, u32[]{:S(2)}, u32[]{:S(2)}) collective-permute-start(bf16[1024,512]{1,0:T(8,128)(2,1)S(1)} %copy-done.5), channel_id=1, source_target_pairs={{0,256},{128,384},{256,0},{384,128},{1,257},{129,385},{257,1},{385... | collective-permute-start | bytes 3145736 | tf_op jit(solution)/shard_map/ppermute | solution.py:341
  84.7 8.2 %copy-start.3 = (bf16[128,512]{1,0:T(8,128)(2,1)S(1)}, bf16[128,512]{1,0:T(8,128)(2,1)}, u32[]{:S(2)}) copy-start(bf16[128,512]{1,0:T(8,128)(2,1)} %query.3) | copy-start | bytes 393220
  85.2 12.2 %collective-permute-start.5 = (bf16[4096,256]{1,0:T(8,128)(2,1)S(1)}, bf16[4096,256]{1,0:T(8,128)(2,1)}, u32[]{:S(2)}, u32[]{:S(2)}) collective-permute-start(bf16[4096,256]{1,0:T(8,128)(2,1)S(1)} %bitcast.13), channel_id=1, source_target_pairs={{0,128},{128,0},{256,384},{384,256},{1,129},{129,1},{257,385},{385... | collective-permute-start | bytes 6291464 | tf_op jit(solution)/shard_map/ppermute | solution.py:338
  92.7 56.8 %all-gather.13.cloned.1.call-start = ((), (), s32[]{:S(2)}) async-start(), calls=%async_computation.4 | async-start | bytes 3145728 | tf_op jit(solution)/shard_map/all_gather | solution.py:362
  130.3 19.1 %all-to-all-start.1 = ((bf16[8,128,512]{2,1,0:T(8,128)(2,1)}), bf16[8,128,512]{2,1,0:T(8,128)(2,1)S(1)}, u32[]{:S(2)}, u32[]{:S(2)}) async-start(bf16[8,128,512]{2,1,0:T(8,128)(2,1)} %get-tuple-element.37), calls=%async_computation.1 | async-start | bytes 2097152 | tf_op jit(solution)/shard_map/all_to_all | solution.py:401
Sparse Core Ops, SparseCore 0:
  10.2 84.5 all-gather.8
  96.9 21.3 all-gather.10
  128.6 18.2 all-gather.12

commit v4 on v3

--- a/solution.py
+++ b/solution.py
@@ -1,3 +1,4 @@
+import functools
 import math
 
 import jax
@@ -10,6 +11,7 @@
 HD = 128
 KV = 2 * HD
 SCALE_ROWS = 16
+HALVES = 1
 TOP = 13.0
 SCORE_SCALE = math.log2(math.e) / math.sqrt(HD)
 
@@ -21,6 +23,10 @@
 SMEM_SPEC = pl.BlockSpec(memory_space=pltpu.SMEM)
 VMEM_SPEC = pl.BlockSpec(memory_space=pltpu.VMEM)
 HBM_SPEC = pl.BlockSpec(memory_space=pltpu.HBM)
+
+
+def in_vmem(value):
+    return pltpu.with_memory_space_constraint(value, pltpu.VMEM)
 
 
 def in_hbm(value):
@@ -121,13 +127,11 @@
     return jnp.concatenate([query[:, g * HD : (g + 1) * HD] for g in range(group)], axis=0)
 
 
-def absorb(state, q, cache, pos, index, first, rows, loads=()):
+def absorb(state, q, cache, pos, index, first, rows):
     highest, total = state
     group = q.shape[0] // rows
     size = pos.shape[1]
     for step in range(cache.shape[0] // size):
-        if loads:
-            loads[step].wait()
         keys = cache[step * size : (step + 1) * size, :HD]
         value = cache[step * size : (step + 1) * size, HD:]
         scores = lax.dot_general(
@@ -192,21 +196,24 @@
 
 
 def first_layer_kernel(
-    place, query, pos, high_in, total_in, mate, weight, out, near, held, stage, mate_sem, sem, out_sem
+    half, place, query, pos, mate, high_in, total_in, weight, out, held, stage, sem, out_sem
 ):
     sections = weight.shape[0]
-    mate_loads = load_rows(mate, near, mate_sem, mate.shape[0] // pos.shape[1])
     loads = load_rows(weight, held, sem, sections)
-    q = stack_heads(query)
-    rows = query.shape[0]
+    heads, rows, share = stage.shape
+    first_row = half * rows
+
+    def mine(value):
+        starts = range(first_row, value.shape[0], query.shape[0])
+        return jnp.concatenate([value[i : i + rows] for i in starts], axis=0)
+
+    q = stack_heads(query[first_row : first_row + rows])
     core = place[0] & 1
-    state = (high_in[:, :1], total_in[...])
-    state = absorb(state, q, near, pos, 1 - core, place[1], rows, mate_loads)
-    attended = finish(state)
+    state = (mine(high_in)[:, :1], mine(total_in))
+    attended = finish(absorb(state, q, mate, pos, 1 - core, place[1] + first_row, rows))
     first = jnp.concatenate(
         [attended[g : g + rows] for g in range(0, attended.shape[0], rows)], axis=1
     )
-    heads, _, share = stage.shape
     each = heads // sections
     stores = []
     for h in range(heads):
@@ -220,26 +227,24 @@
         store.wait()
 
 
-def first_layer(place, query, pos, state, mate, weight, heads):
-    rows = query.shape[0]
+def first_layer(half, place, query, pos, mate, state, weight, heads):
+    rows = query.shape[0] // HALVES
     sections, _, width = weight.shape
     shape = (heads, rows, sections * width // heads)
     return pl.pallas_call(
-        first_layer_kernel,
+        functools.partial(first_layer_kernel, half),
         out_shape=pltpu.HBM(shape, jnp.bfloat16),
-        in_specs=[SMEM_SPEC] + [VMEM_SPEC] * 4 + [HBM_SPEC] * 2,
+        in_specs=[SMEM_SPEC] + [VMEM_SPEC] * 5 + [HBM_SPEC],
         out_specs=HBM_SPEC,
         scratch_shapes=[
-            pltpu.VMEM(mate.shape, jnp.bfloat16),
             pltpu.VMEM(weight.shape, jnp.bfloat16),
             pltpu.VMEM(shape, jnp.bfloat16),
-            pltpu.SemaphoreType.DMA((mate.shape[0] // pos.shape[1],)),
             pltpu.SemaphoreType.DMA((sections,)),
             pltpu.SemaphoreType.DMA((heads,)),
         ],
-        compiler_params=limit(32),
+        compiler_params=limit(28),
         name="first_layer",
-    )(place, query, pos, *state, in_hbm(mate), in_hbm(weight))
+    )(place, query, pos, in_vmem(mate), *state, in_hbm(weight))
 
 
 def residual_kernel(pieces, hidden, gain, stream, spread, scaled, sem):
@@ -276,53 +281,39 @@
 
 
 def second_layer_kernel(
-    place, scaled, inverse, pos, own, near, far, mate, out, held, other, sem, mate_sem
+    half, place, scaled, inverse, pos, own, mate, near, far, out
 ):
     heads, rows, share = scaled.shape
-    half = heads // 2
-    each = half // near.shape[0]
+    group = heads // 2
+    each = group // near.shape[0]
     core, side = place[0] & 1, place[0] >> 1
-    loads = [
-        load_rows(weight, held.at[i], sem.at[i], weight.shape[0])
-        for i, weight in enumerate((near, far))
-    ]
-    mate_loads = load_rows(mate, other, mate_sem, mate.shape[0] // pos.shape[1])
     square = jnp.zeros((rows, 1), jnp.float32)
     for h in range(heads):
         plain = scaled[h].astype(jnp.float32) * inverse[h : h + 1]
         square = square + jnp.sum(plain * plain, axis=1, keepdims=True)
     root = lax.rsqrt(square / (heads * share) + 1e-6)
     total = jnp.zeros((rows, near.shape[2]), jnp.float32)
-    for i in range(2):
-        for k in range(half):
-            if k % each == 0:
-                loads[i][k // each].wait()
-            part = held[i, k // each, (k % each) * share : (k % each + 1) * share]
-            total = total + dot(scaled[(side ^ i) * half + k], part)
+    for i, weight in enumerate((near, far)):
+        for k in range(group):
+            part = weight[k // each, (k % each) * share : (k % each + 1) * share]
+            total = total + dot(scaled[(side ^ i) * group + k], part)
     q = stack_heads((total * root).astype(jnp.bfloat16))
-    state = absorb(fresh(q), q, own, pos, core, place[1], rows)
-    state = absorb(state, q, other, pos, 1 - core, place[1], rows, mate_loads)
-    attended = finish(state)
+    first_pos = place[1] + half * rows
+    state = absorb(fresh(q), q, own, pos, core, first_pos, rows)
+    attended = finish(absorb(state, q, mate, pos, 1 - core, first_pos, rows))
     for g in range(out.shape[1] // HD):
         out[:, g * HD : (g + 1) * HD] = attended[g * rows : (g + 1) * rows]
 
 
-def second_layer(place, scaled, inverse, pos, own, near, far, mate):
-    parts = mate.shape[0] // pos.shape[1]
-    return pl.pallas_call(
-        second_layer_kernel,
+def second_layer(half, place, scaled, inverse, pos, own, mate, near, far):
+    return pl.pallas_call(
+        functools.partial(second_layer_kernel, half),
         out_shape=jax.ShapeDtypeStruct((scaled.shape[1], near.shape[2]), jnp.bfloat16),
-        in_specs=[SMEM_SPEC] + [VMEM_SPEC] * 4 + [HBM_SPEC] * 3,
+        in_specs=[SMEM_SPEC] + [VMEM_SPEC] * 7,
         out_specs=VMEM_SPEC,
-        scratch_shapes=[
-            pltpu.VMEM((2,) + near.shape, jnp.bfloat16),
-            pltpu.VMEM(mate.shape, jnp.bfloat16),
-            pltpu.SemaphoreType.DMA((2, near.shape[0])),
-            pltpu.SemaphoreType.DMA((parts,)),
-        ],
-        compiler_params=limit(36),
+        compiler_params=limit(28),
         name="second_layer",
-    )(place, scaled, inverse, pos, own, in_hbm(near), in_hbm(far), in_hbm(mate))
+    )(place, scaled, inverse, pos, own, in_vmem(mate), in_hbm(near), in_hbm(far))
 
 
 def per_device(
@@ -369,8 +360,6 @@
         (near_columns, far_columns, kv_weight)
     )
     mate_weight = swap_core(moved_weight)
-    own_hidden = lax.dynamic_slice_in_dim(self_hidden, head * share, share, 1)
-    mate_weight, own_hidden = lax.optimization_barrier((mate_weight, own_hidden))
     own = kv_own(here, self_hidden, kv_weight, mate_weight)
     own, send = kv_near(own, from_near, from_far, kv_weight, mate_weight)
     other = swap_y(send)
@@ -393,14 +382,15 @@
     cache_own = cache_own.reshape(ctxs * 2 * rows, KV)
     cache_mate = swap_core(cache_own)
     state = own_keys(place, queries, pos, cache_own)
-    partial = first_layer(place, queries, pos, state, cache_mate, out_all, heads)
+    partial = first_layer(0, place, queries, pos, cache_mate, state, out_all, heads)
+    partial, late_hidden, query_far = lax.optimization_barrier((partial, self_hidden, query_far))
+    own_hidden = lax.dynamic_slice_in_dim(late_hidden, head * share, share, 1)
     pieces = lax.all_to_all(partial, "head", 0, 0, tiled=True)
-    pieces, query_far = lax.optimization_barrier((pieces, query_far))
     query_far = pair(query_far)
     stream, spread = residual_sum(pieces, own_hidden, own_gain)
     scaled_all = lax.all_to_all(spread, "head", 0, 0, tiled=True)
     second = second_layer(
-        place, scaled_all, inverse, pos, cache_own, query_near, query_far, cache_mate
+        0, place, scaled_all, inverse, pos, cache_own, cache_mate, query_near, query_far
     )
     return (stream, second)
 

time: 170 us -> 165 us (0.971)
  blocking collectives: 61.7 us -> 40.9 us
  waiting for transfers between devices: 26.7 us -> 43.3 us
  Pallas kernels: 30.5 us -> 25.8 us
  starting transfers between devices: 29.5 us -> 33.4 us
    all_to_all x1 -> x0, blocking collectives: 20.8 us -> none  [per_device(): pieces = lax.all_to_all(partial, 'head', 0, 0, tiled=True)]
    all_to_all x0 -> x1, waiting for transfers between devices: none -> 15.7 us  [per_device(): pieces = lax.all_to_all(partial, 'head', 0, 0, tiled=True)]
    pallas_call x2, Pallas kernels: 23.3 us -> 18.5 us  [the longest x1 10.8 us: second_layer(): pl.pallas_call(functools.partial(second_layer_kernel, half), out_shape=ja...]
    all_to_all x0 -> x1, starting transfers between devices: none -> 4.09 us  [per_device(): pieces = lax.all_to_all(partial, 'head', 0, 0, tiled=True)]
  transfers between devices with their start and end apart: 10 -> 11, of which waited for: 5 -> 6; matrix products, arithmetic and copies ran while one was open for 3% -> 3% of each run, Pallas kernels for 10% -> 9%
where the time goes in v4:
time: 165 us; the launch traced here: 164 us
  waiting for transfers between devices  43.3 us (26%)
  blocking collectives  40.9 us (25%)
  starting transfers between devices  33.4 us (20%)
  Pallas kernels  25.8 us (16%)
  between operations  14.1 us (9%)
  local copies, waits for them, and re-layouts  5.01 us (3%)
    all_gather x1, blocking collectives, per_device(): coded = lax.all_gather(turned, 'ctx', axis=0)  40.9 us
    ppermute x2, starting transfers between devices, swap_core(): return lax.ppermute(value, 'section', [(i, i ^ 1) for i in range(sections)])  16.3 us
    all_to_all x1, waiting for transfers between devices, per_device(): pieces = lax.all_to_all(partial, 'head', 0, 0, tiled=True)  15.7 us
    all_to_all x1, waiting for transfers between devices, per_device(): scaled_all = lax.all_to_all(spread, 'head', 0, 0, tiled=True)  15.3 us
    pallas_call x1, Pallas kernels, second_layer(): pl.pallas_call(functools.partial(second_layer_kernel, half), out_shape=ja...  10.8 us
    ppermute x3, waiting for transfers between devices, swap_y(): return lax.ppermute(value, 'section', [(i, i ^ 2) for i in range(sections)])  8.43 us
    pallas_call x1, Pallas kernels, first_layer(): pl.pallas_call(functools.partial(first_layer_kernel, half), out_shape=plt...  7.69 us
    ppermute x3, starting transfers between devices, swap_y(): return lax.ppermute(value, 'section', [(i, i ^ 2) for i in range(sections)])  7.19 us
  transfers between devices with their start and end apart: 11, of which 6 were waited for; matrix products, arithmetic and copies ran while one was open for 3% of the time, Pallas kernels for 9%

profile of v4, /device:TPU:1, one launch (start us, length us, event | category | flops | bytes accessed | tf_op | source)
XLA Modules:
  0.0 164.0 jit_solution(1093177771546508120)
XLA Ops:
  7.3 0.7 all-gather.9.cloned.1.call-update
  8.0 1.1 constant_dynamic-slice_fusion.1
  9.1 8.8 %collective-permute-start = (bf16[1024,256]{1,0:T(8,128)(2,1)}, bf16[1024,256]{1,0:T(8,128)(2,1)S(1)}, u32[]{:S(2)}, u32[]{:S(2)}) collective-permute-start(bf16[1024,256]{1,0:T(8,128)(2,1)} %weight.3), channel_id=1, source_target_pairs={{0,128},{128,0},{256,384},{384,256},{1,129},{129,1},{257,385},{385... | collective-permute-start | bytes 1572872 | tf_op jit(solution)/shard_map/ppermute | solution.py:329
  17.9 1.9 %collective-permute-start.1 = (bf16[128,1024]{1,0:T(8,128)(2,1)S(1)}, bf16[128,1024]{1,0:T(8,128)(2,1)S(1)}, u32[]{:S(2)}, u32[]{:S(2)}) collective-permute-start(bf16[128,1024]{1,0:T(8,128)(2,1)S(1)} %get-tuple-element.39), channel_id=1, source_target_pairs={{0,256},{128,384},{256,0},{384,128},{1,257},{129,385},{257,1},{385... | collective-permute-start | bytes 786440 | tf_op jit(solution)/shard_map/ppermute | solution.py:332
  19.8 1.9 %collective-permute-start.2 = (bf16[128,1024]{1,0:T(8,128)(2,1)S(1)}, bf16[128,1024]{1,0:T(8,128)(2,1)S(1)}, u32[]{:S(2)}, u32[]{:S(2)}) collective-permute-start(bf16[128,1024]{1,0:T(8,128)(2,1)S(1)} %get-tuple-element.38), channel_id=1, source_target_pairs={{0,257},{1,256},{2,259},{3,258},{4,261},{5,260},{6,263},{7,262},{1... | collective-permute-start | bytes 786440 | tf_op jit(solution)/shard_map/ppermute | solution.py:340
  21.8 1.2 copy-done
  23.0 1.0 copy-done.1
  24.0 0.3 kv_own.1.own
  24.3 3.4 %collective-permute-done.1.from_near = bf16[128,1024]{1,0:T(8,128)(2,1)S(1)} collective-permute-done((bf16[128,1024]{1,0:T(8,128)(2,1)S(1)}, bf16[128,1024]{1,0:T(8,128)(2,1)S(1)}, u32[]{:S(2)}, u32[]{:S(2)}) %collective-permute-start.1) | collective-permute-done | bytes 262176 | tf_op jit(solution)/shard_map/ppermute | solution.py:332
  27.7 3.1 %collective-permute-done.2.from_far = bf16[128,1024]{1,0:T(8,128)(2,1)S(1)} collective-permute-done((bf16[128,1024]{1,0:T(8,128)(2,1)S(1)}, bf16[128,1024]{1,0:T(8,128)(2,1)S(1)}, u32[]{:S(2)}, u32[]{:S(2)}) %collective-permute-start.2) | collective-permute-done | bytes 262176 | tf_op jit(solution)/shard_map/ppermute | solution.py:340
  30.8 0.3 kv_near.1
  31.2 1.9 %collective-permute-start.3 = (bf16[256,256]{1,0:T(8,128)(2,1)S(1)}, bf16[256,256]{1,0:T(8,128)(2,1)S(1)}, u32[]{:S(2)}, u32[]{:S(2)}) collective-permute-start(bf16[256,256]{1,0:T(8,128)(2,1)S(1)} %get-tuple-element.21), channel_id=1, source_target_pairs={{0,256},{128,384},{256,0},{384,128},{1,257},{129,385},{257,1},{385... | collective-permute-start | bytes 393224 | tf_op jit(solution)/shard_map/ppermute | solution.py:332
  33.1 0.6 dynamic_slice.18
  33.7 3.4 %collective-permute-start.4 = (bf16[1024,512]{1,0:T(8,128)(2,1)S(1)}, bf16[1024,512]{1,0:T(8,128)(2,1)}, u32[]{:S(2)}, u32[]{:S(2)}) collective-permute-start(bf16[1024,512]{1,0:T(8,128)(2,1)S(1)} %copy-done.5), channel_id=1, source_target_pairs={{0,256},{128,384},{256,0},{384,128},{1,257},{129,385},{257,1},{385... | collective-permute-start | bytes 3145736 | tf_op jit(solution)/shard_map/ppermute | solution.py:332
  37.1 0.7 pad_add_fusion.place
  37.8 0.1 dynamic_slice.19
  38.0 1.3 collective-permute-done.3.other
  39.3 0.3 rotate.1
  39.7 40.9 %all-gather.14 = f16[4352,256]{1,0:T(8,128)(2,1)S(1)} all-gather(f16[272,256]{1,0:T(8,128)(2,1)S(1)} %convert_element_type.13), channel_id=2, replica_groups=mesh['section'=4,'ctx'=16,'head'=8] {'ctx'}, dimensions={0}, use_global_device_ids=true | all-gather | bytes 2367488 | tf_op jit(solution)/shard_map/all_gather | solution.py:377
  80.5 3.7 %collective-permute-done.4 = bf16[1024,512]{1,0:T(8,128)(2,1)} collective-permute-done((bf16[1024,512]{1,0:T(8,128)(2,1)S(1)}, bf16[1024,512]{1,0:T(8,128)(2,1)}, u32[]{:S(2)}, u32[]{:S(2)}) %collective-permute-start.4) | collective-permute-done | bytes 1048608 | tf_op jit(solution)/shard_map/ppermute | solution.py:332
  84.2 0.4 convert_element_type.14
  84.8 0.4 fusion
  85.2 7.5 %collective-permute-start.5 = (bf16[4096,256]{1,0:T(8,128)(2,1)S(1)}, bf16[4096,256]{1,0:T(8,128)(2,1)}, u32[]{:S(2)}, u32[]{:S(2)}) collective-permute-start(bf16[4096,256]{1,0:T(8,128)(2,1)S(1)} %bitcast.13), channel_id=1, source_target_pairs={{0,128},{128,0},{256,384},{384,256},{1,129},{129,1},{257,385},{385... | collective-permute-start | bytes 6291464 | tf_op jit(solution)/shard_map/ppermute | solution.py:329
  92.8 4.5 %own_keys.1 = (f32[512,128]{1,0:T(8,128)S(1)}, f32[512,256]{1,0:T(8,128)S(1)}) custom-call(s32[2]{0:T(128)S(1)} %pad_add_fusion.place, bf16[128,512]{1,0:T(8,128)(2,1)S(1)} %copy-done.3, s32[4,2048]{1,0:T(4,128)S(1)} %reshape.24.pos, bf16[4096,256]{1,0:T(8,128)(2,1)S(1)} %bitcast.14), custom_call_target="tpu_custom_call" | custom-call | tf_op jit(solution)/shard_map/own_keys/pallas_call | solution.py:185
  97.3 7.7 %first_layer.1 = bf16[8,128,512]{2,1,0:T(8,128)(2,1)} custom-call(s32[2]{0:T(128)S(1)} %pad_add_fusion.place, bf16[128,512]{1,0:T(8,128)(2,1)S(1)} %copy-done.3, s32[4,2048]{1,0:T(4,128)S(1)} %reshape.24.pos, bf16[4096,256]{1,0:T(8,128)(2,1)} %collective-permute-done.5.mate, f32[512,128]{1,0:T(8,128)S(1)} %get-tuple-element.28.high_in, ...), custom_call_target="tpu_custom_call" | custom-call | tf_op jit(solution)/shard_map/first_layer/pallas_call | solution.py:234
  105.0 4.1 %all-to-all-start = ((bf16[8,128,512]{2,1,0:T(8,128)(2,1)}), bf16[8,128,512]{2,1,0:T(8,128)(2,1)S(1)}, u32[]{:S(2)}, u32[]{:S(2)}) async-start(bf16[8,128,512]{2,1,0:T(8,128)(2,1)} %first_layer.1), calls=%async_computation | async-start | bytes 2097152 | tf_op jit(solution)/shard_map/all_to_all | solution.py:388
  109.1 0.9 constant_dynamic-slice_fusion.hidden
  110.0 15.7 %all-to-all-done.pieces = bf16[8,128,512]{2,1,0:T(8,128)(2,1)S(1)} async-done(((bf16[8,128,512]{2,1,0:T(8,128)(2,1)}), bf16[8,128,512]{2,1,0:T(8,128)(2,1)S(1)}, u32[]{:S(2)}, u32[]{:S(2)}) %all-to-all-start) | async-done | bytes 1048608 | tf_op jit(solution)/shard_map/all_to_all | solution.py:388
  125.7 1.9 %residual_sum.1 = (bf16[128,512]{1,0:T(8,128)(2,1)}, bf16[8,128,512]{2,1,0:T(8,128)(2,1)}) custom-call(bf16[8,128,512]{2,1,0:T(8,128)(2,1)S(1)} %all-to-all-done.pieces, bf16[128,512]{1,0:T(8,128)(2,1)S(1)} %constant_dynamic-slice_fusion.hidden, f32[1,512]{1,0:T(1,128)S(1)} %bitcast.16), custom_call_target="tpu_custom_call" | custom-call | tf_op jit(solution)/shard_map/residual_sum/pallas_call | solution.py:266
  127.6 3.7 %all-to-all-start.1 = ((bf16[8,128,512]{2,1,0:T(8,128)(2,1)}), bf16[8,128,512]{2,1,0:T(8,128)(2,1)S(1)}, u32[]{:S(2)}, u32[]{:S(2)}) async-start(bf16[8,128,512]{2,1,0:T(8,128)(2,1)} %get-tuple-element.35), calls=%async_computation.1 | async-start | bytes 2097152 | tf_op jit(solution)/shard_map/all_to_all | solution.py:391
  131.3 15.3 %all-to-all-done.1.scaled = bf16[8,128,512]{2,1,0:T(8,128)(2,1)S(1)} async-done(((bf16[8,128,512]{2,1,0:T(8,128)(2,1)}), bf16[8,128,512]{2,1,0:T(8,128)(2,1)S(1)}, u32[]{:S(2)}, u32[]{:S(2)}) %all-to-all-start.1) | async-done | bytes 1048608 | tf_op jit(solution)/shard_map/all_to_all | solution.py:391
  146.7 10.8 %second_layer.1 = bf16[128,512]{1,0:T(8,128)(2,1)} custom-call(s32[2]{0:T(128)S(1)} %pad_add_fusion.place, bf16[8,128,512]{2,1,0:T(8,128)(2,1)S(1)} %all-to-all-done.1.scaled, f32[8,512]{1,0:T(8,128)S(1)} %reshape.26.inverse, s32[4,2048]{1,0:T(4,128)S(1)} %reshape.24.pos, bf16[4096,256]{1,0:T(8,128)(2,1)S(1)} %bitcast.15, ...), custom_call_target="tpu_custom_call" | custom-call | tf_op jit(solution)/shard_map/second_layer/pallas_call | solution.py:309
  (31 shorter events, 0.4 us)
Async XLA Ops:
  7.2 23.7 %copy-start.2 = (bf16[1024,256]{1,0:T(8,128)(2,1)S(1)}, bf16[1024,256]{1,0:T(8,128)(2,1)}, u32[]{:S(2)}) copy-start(bf16[1024,256]{1,0:T(8,128)(2,1)} %weight.3) | copy-start | bytes 1572868
  7.2 25.9 %copy-start.7 = (bf16[4096]{0:T(1024)(128)(2,1)S(1)}, bf16[4096]{0:T(1024)(128)(2,1)}, u32[]{:S(2)}) copy-start(bf16[4096]{0:T(1024)(128)(2,1)} %param.15) | copy-start | bytes 24580
  7.2 25.9 %copy-start.6 = (s32[8192]{0:T(1024)S(1)}, s32[8192]{0:T(1024)}, u32[]{:S(2)}) copy-start(s32[8192]{0:T(1024)} %param.11) | copy-start | bytes 98308
  7.2 26.5 %copy-start.5 = (bf16[1024,512]{1,0:T(8,128)(2,1)S(1)}, bf16[1024,512]{1,0:T(8,128)(2,1)}, u32[]{:S(2)}) copy-start(bf16[1024,512]{1,0:T(8,128)(2,1)} %param.14) | copy-start | bytes 3145732
  7.2 32.1 %copy-start.4 = (s32[1,128]{1,0:T(1,128)S(1)}, s32[1,128]{1,0:T(1,128)}, u32[]{:S(2)}) copy-start(s32[1,128]{1,0:T(1,128)} %signs.1) | copy-start | bytes 1540
  7.2 90.1 %all-gather.9.cloned.1.call-start = ((), (), s32[]{:S(2)}) async-start(), calls=%async_computation.2 | async-start | bytes 5242880 | tf_op jit(solution)/shard_map/all_gather | solution.py:366
  8.0 123.4 %all-gather.11.cloned.1.call-start = ((), (), s32[]{:S(2)}) async-start(), calls=%async_computation.3 | async-start | bytes 3145728 | tf_op jit(solution)/shard_map/all_gather | solution.py:353
  9.1 12.7 %collective-permute-start = (bf16[1024,256]{1,0:T(8,128)(2,1)}, bf16[1024,256]{1,0:T(8,128)(2,1)S(1)}, u32[]{:S(2)}, u32[]{:S(2)}) collective-permute-start(bf16[1024,256]{1,0:T(8,128)(2,1)} %weight.3), channel_id=1, source_target_pairs={{0,128},{128,0},{256,384},{384,256},{1,129},{129,1},{257,385},{385... | collective-permute-start | bytes 1572872 | tf_op jit(solution)/shard_map/ppermute | solution.py:329
  17.9 9.8 %collective-permute-start.1 = (bf16[128,1024]{1,0:T(8,128)(2,1)S(1)}, bf16[128,1024]{1,0:T(8,128)(2,1)S(1)}, u32[]{:S(2)}, u32[]{:S(2)}) collective-permute-start(bf16[128,1024]{1,0:T(8,128)(2,1)S(1)} %get-tuple-element.39), channel_id=1, source_target_pairs={{0,256},{128,384},{256,0},{384,128},{1,257},{129,385},{257,1},{385... | collective-permute-start | bytes 786440 | tf_op jit(solution)/shard_map/ppermute | solution.py:332
  19.8 11.0 %collective-permute-start.2 = (bf16[128,1024]{1,0:T(8,128)(2,1)S(1)}, bf16[128,1024]{1,0:T(8,128)(2,1)S(1)}, u32[]{:S(2)}, u32[]{:S(2)}) collective-permute-start(bf16[128,1024]{1,0:T(8,128)(2,1)S(1)} %get-tuple-element.38), channel_id=1, source_target_pairs={{0,257},{1,256},{2,259},{3,258},{4,261},{5,260},{6,263},{7,262},{1... | collective-permute-start | bytes 786440 | tf_op jit(solution)/shard_map/ppermute | solution.py:340
  21.8 1.2 copy-start
  23.0 1.0 copy-start.1
  31.2 8.1 %collective-permute-start.3 = (bf16[256,256]{1,0:T(8,128)(2,1)S(1)}, bf16[256,256]{1,0:T(8,128)(2,1)S(1)}, u32[]{:S(2)}, u32[]{:S(2)}) collective-permute-start(bf16[256,256]{1,0:T(8,128)(2,1)S(1)} %get-tuple-element.21), channel_id=1, source_target_pairs={{0,256},{128,384},{256,0},{384,128},{1,257},{129,385},{257,1},{385... | collective-permute-start | bytes 393224 | tf_op jit(solution)/shard_map/ppermute | solution.py:332
  33.7 50.5 %collective-permute-start.4 = (bf16[1024,512]{1,0:T(8,128)(2,1)S(1)}, bf16[1024,512]{1,0:T(8,128)(2,1)}, u32[]{:S(2)}, u32[]{:S(2)}) collective-permute-start(bf16[1024,512]{1,0:T(8,128)(2,1)S(1)} %copy-done.5), channel_id=1, source_target_pairs={{0,256},{128,384},{256,0},{384,128},{1,257},{129,385},{257,1},{385... | collective-permute-start | bytes 3145736 | tf_op jit(solution)/shard_map/ppermute | solution.py:332
  84.7 8.1 %copy-start.3 = (bf16[128,512]{1,0:T(8,128)(2,1)S(1)}, bf16[128,512]{1,0:T(8,128)(2,1)}, u32[]{:S(2)}) copy-start(bf16[128,512]{1,0:T(8,128)(2,1)} %query.3) | copy-start | bytes 393220
  85.2 12.1 %collective-permute-start.5 = (bf16[4096,256]{1,0:T(8,128)(2,1)S(1)}, bf16[4096,256]{1,0:T(8,128)(2,1)}, u32[]{:S(2)}, u32[]{:S(2)}) collective-permute-start(bf16[4096,256]{1,0:T(8,128)(2,1)S(1)} %bitcast.13), channel_id=1, source_target_pairs={{0,128},{128,0},{256,384},{384,256},{1,129},{129,1},{257,385},{385... | collective-permute-start | bytes 6291464 | tf_op jit(solution)/shard_map/ppermute | solution.py:329
  92.7 54.0 %all-gather.13.cloned.1.call-start = ((), (), s32[]{:S(2)}) async-start(), calls=%async_computation.4 | async-start | bytes 3145728 | tf_op jit(solution)/shard_map/all_gather | solution.py:353
  105.0 20.7 %all-to-all-start = ((bf16[8,128,512]{2,1,0:T(8,128)(2,1)}), bf16[8,128,512]{2,1,0:T(8,128)(2,1)S(1)}, u32[]{:S(2)}, u32[]{:S(2)}) async-start(bf16[8,128,512]{2,1,0:T(8,128)(2,1)} %first_layer.1), calls=%async_computation | async-start | bytes 2097152 | tf_op jit(solution)/shard_map/all_to_all | solution.py:388
  127.6 19.1 %all-to-all-start.1 = ((bf16[8,128,512]{2,1,0:T(8,128)(2,1)}), bf16[8,128,512]{2,1,0:T(8,128)(2,1)S(1)}, u32[]{:S(2)}, u32[]{:S(2)}) async-start(bf16[8,128,512]{2,1,0:T(8,128)(2,1)} %get-tuple-element.35), calls=%async_computation.1 | async-start | bytes 2097152 | tf_op jit(solution)/shard_map/all_to_all | solution.py:391
Sparse Core Ops, SparseCore 0:
  10.2 84.6 all-gather.8
  96.9 21.3 all-gather.10
  120.4 22.3 all-gather.12
